TPU v7x, 256 devices: a whole 4x4x8 slice. The times are simulated.
256 devices in a mesh: dp: 64 (over x, z, core), mp: 4 (over y).
Axes of the slice: x: 4, y: 4, z: 8, core: 2. Of those that a mesh axis runs over, the one named last changes fastest.
Arguments:
- waveform: bfloat16 [64, 4, 4, 41216], P('dp', 'mp'), may hold values from -6 to 6
- lengths: int32 [64, 4, 4], P('dp', 'mp'), may hold values from 1 to 63, as said below
- conv_first: bfloat16 [64, 1, 3, 3], replicated, may hold values from -2 to 2
- conv_second: bfloat16 [64, 64, 3, 3], replicated, may hold values from -0.25 to 0.25
- input_weight: bfloat16 [1280, 1536], replicated, may hold values from -0.15625 to 0.15625
- norm_gain: float32 [1536], replicated, may hold values from 0.1 to 1.9
- attention_in: bfloat16 [1536, 3, 1536], P(None, None, 'mp'), may hold values from -5.1031036 to 5.1031036
- attention_out: bfloat16 [1536, 1536], P('mp'), may hold values from -0.15625 to 0.15625
- send_slots: int32 [64, 64, 4, 4], P('dp', None, 'mp'), may hold values from -1 to 254, as said below
- receive_slots: int32 [64, 4, 128], P('dp', 'mp'), may hold values from 0 to 255, as said below
- segment_ids: int32 [64, 4, 128], P('dp'), may hold values from 0 to 1023, as said below
Outputs:
- encoded: bfloat16 [64, 4, 128, 1536], P('dp', 'mp')
Inputs may be any that keep to these rules, and one draw needn't show every extreme that they name: `lengths`: in every draw one utterance of each lane m has 63 frames and one has 1. send_slots[i, j, m, c] is the row u * 64 + s of loader (i, m) carried in slot c to packed shard (j, m), or -1 for an empty slot; every frame s below its utterance's length is sent exactly once, and each loader sends at most 4 rows to one packed shard, exactly 4 in some cases of every draw. Each packed shard (j, m) receives exactly 128 rows, only from loaders (i, m); receive_slots[j, m, p] = i * 4 + c names a filled slot, each filled slot once, in order of loader i and then of the loader's rows. `segment_ids`: the id of utterance u of loader (i, m) is (m * 64 + i) * 4 + u; rows with equal ids of a group are consecutive and lie in one device's rows.
All inputs are finite; a program needn't handle non-finite values.
Results may differ from a plain program's by a relative error of at most 0.019.
Values may be sent and summed in bfloat16 or wider, within the bound.
A program may use at most 128 MiB of HBM per device.

v0:
```python
import math

import jax
import jax.numpy as jnp
from jax import lax
from jax.sharding import PartitionSpec as P

N_MEL = 80
N_FFT = 400
HOP = 160
HEAD_DIM = 64
SLOT_ROWS = 64


sample_rate = 16000.0
log_offset = 0.01


def hann_window(length):
    position = jnp.arange(length, dtype=jnp.float32)
    return 0.5 - 0.5 * jnp.cos(2.0 * math.pi * position / length)


def mel_weights(bin_count, window_size, channels):
    frequency = jnp.arange(bin_count, dtype=jnp.float32) * (sample_rate / window_size)
    mel_top = 2595.0 * math.log10(1.0 + 0.5 * sample_rate / 700.0)
    points = jnp.arange(channels + 2, dtype=jnp.float32) * (mel_top / (channels + 1))
    hertz_points = 700.0 * (jnp.power(10.0, points / 2595.0) - 1.0)
    lower_edge = hertz_points[:-2]
    centre = hertz_points[1:-1]
    upper_edge = hertz_points[2:]
    rising = (frequency[:, None] - lower_edge[None, :]) / (centre - lower_edge)[None, :]
    falling = (upper_edge[None, :] - frequency[:, None]) / (upper_edge - centre)[None, :]
    return jnp.maximum(0.0, jnp.minimum(rising, falling))


def frame_signal(signal, hop_size, window_size, frame_count):
    pieces = -(-window_size // hop_size)
    needed = hop_size * (frame_count + pieces)
    extra_zeros = max(needed - signal.shape[-1], 0)
    padded = jnp.pad(signal, ((0, 0), (0, extra_zeros)))
    blocks = padded.reshape(signal.shape[0], frame_count + pieces, hop_size)
    joined = jnp.concatenate(
        [blocks[:, offset : offset + frame_count, :] for offset in range(pieces)], axis=-1
    )
    return joined[:, :, :window_size]


def log_mel(signal, own_lengths, hop_size, window_size, channels, frame_count):
    frames = frame_signal(signal, hop_size, window_size, frame_count)
    bin_count = window_size // 2 + 1
    padded_bins = -(-bin_count // 128) * 128
    position = jnp.arange(window_size, dtype=jnp.float32)[:, None]
    harmonic = jnp.arange(padded_bins, dtype=jnp.float32)[None, :]
    angles = 2.0 * math.pi * jnp.mod(position * harmonic, window_size) / window_size
    inside = harmonic < bin_count
    unit_scale = 1.0 / math.sqrt(window_size)
    window_column = hann_window(window_size)[:, None] * unit_scale
    dft_table = (
        jnp.concatenate(
            [jnp.where(inside, jnp.cos(angles), 0.0), jnp.where(inside, -jnp.sin(angles), 0.0)],
            axis=1,
        )
        * window_column
    )
    table_high = lax.optimization_barrier(dft_table.astype(jnp.bfloat16))
    table_low = (dft_table - table_high.astype(jnp.float32)).astype(jnp.bfloat16)
    spectrum = jnp.einsum("ufn,nk->ufk", frames, table_high, preferred_element_type=jnp.float32)
    spectrum = spectrum + jnp.einsum(
        "ufn,nk->ufk", frames, table_low, preferred_element_type=jnp.float32
    )
    power_bins = spectrum[..., :padded_bins] ** 2 + spectrum[..., padded_bins:] ** 2
    weights = jnp.pad(
        mel_weights(bin_count, window_size, channels), ((0, padded_bins - bin_count), (0, 0))
    )
    energy = jnp.einsum("ufk,km->umf", power_bins, weights, precision=lax.Precision.HIGHEST)
    audible = (
        jnp.arange(frame_count, dtype=jnp.int32)[None, None, :] < 4 * own_lengths[:, None, None]
    )
    return jnp.where(audible, jnp.log(energy + log_offset), 0.0).astype(jnp.bfloat16)


def subsample(log_image, conv_first, conv_second):
    numbers = ("NCHW", "OIHW", "NCHW")
    hidden = lax.conv_general_dilated(
        log_image[:, None],
        conv_first,
        (2, 2),
        ((1, 1), (1, 1)),
        dimension_numbers=numbers,
        preferred_element_type=jnp.float32,
    )
    hidden = jnp.maximum(hidden, 0.0).astype(jnp.bfloat16)
    output = lax.conv_general_dilated(
        hidden,
        conv_second,
        (2, 2),
        ((1, 1), (1, 1)),
        dimension_numbers=numbers,
        preferred_element_type=jnp.float32,
    )
    output = jnp.maximum(output, 0.0).astype(jnp.bfloat16)
    utterances, channels, mel_bands, steps = output.shape
    return output.transpose(0, 3, 1, 2).reshape(utterances * steps, channels * mel_bands)


def layer_norm(inputs, norm_gain):
    values = inputs.astype(jnp.float32)
    centre = values - jnp.mean(values, axis=-1, keepdims=True)
    spread = jnp.mean(centre * centre, axis=-1, keepdims=True)
    return (centre * lax.rsqrt(spread + 1e-05) * norm_gain).astype(jnp.bfloat16)


def attend(queries, key_rows, value_rows, row_ids, head_size):
    scores = jnp.einsum(
        "qhd,khd->hqk", queries, key_rows, preferred_element_type=jnp.float32
    ) / math.sqrt(head_size)
    same_segment = row_ids[:, None] == row_ids[None, :]
    scores = jnp.where(same_segment[None], scores, -jnp.inf)
    largest = jnp.max(scores, axis=-1, keepdims=True)
    exponent = jnp.exp(scores - largest)
    attention_weights = (exponent / jnp.sum(exponent, axis=-1, keepdims=True)).astype(jnp.bfloat16)
    context = jnp.einsum(
        "hqk,khd->qhd", attention_weights, value_rows, preferred_element_type=jnp.float32
    )
    return context.astype(jnp.bfloat16).reshape(queries.shape[0], -1)


def on_device(
    waveform,
    lengths,
    conv_first,
    conv_second,
    input_weight,
    norm_gain,
    attention_in,
    attention_out,
    send_slots,
    receive_slots,
    segment_ids,
):
    signal = waveform[0, 0]
    own_lengths = lengths[0, 0]
    log_image = log_mel(signal, own_lengths, HOP, N_FFT, N_MEL, 4 * SLOT_ROWS)
    features = subsample(log_image, conv_first, conv_second)
    slot_table = send_slots[0, :, 0, :]
    fanout = slot_table.shape[0]
    capacity = slot_table.shape[1]
    picked = jnp.maximum(slot_table, 0).reshape(-1)
    arrivals = receive_slots[0, 0]
    embedded = jnp.dot(features, input_weight, preferred_element_type=jnp.float32).astype(
        jnp.bfloat16
    )
    outgoing = jnp.take(embedded, picked, axis=0).reshape(fanout, capacity, embedded.shape[1])
    incoming = lax.all_to_all(outgoing, "dp", split_axis=0, concat_axis=0, tiled=True)
    packed = jnp.take(incoming.reshape(fanout * capacity, embedded.shape[1]), arrivals, axis=0)
    tok_rows = packed.shape[0]
    model_width = packed.shape[1]
    normed = layer_norm(packed, norm_gain)
    local_width = attention_in.shape[2]
    projector = attention_in.reshape(model_width, 3 * local_width)
    projected = jnp.dot(
        lax.all_gather(normed, "mp", axis=0, tiled=True),
        projector,
        preferred_element_type=jnp.float32,
    ).astype(jnp.bfloat16)
    group_ids = segment_ids[0].reshape(-1)
    group_count = projected.shape[0]
    local_heads = local_width // HEAD_DIM
    heads_view = projected.reshape(group_count, 3, local_heads, HEAD_DIM)
    contexts = attend(heads_view[:, 0], heads_view[:, 1], heads_view[:, 2], group_ids, HEAD_DIM)
    attended = lax.psum_scatter(
        jnp.dot(contexts, attention_out, preferred_element_type=jnp.float32).astype(jnp.bfloat16),
        "mp",
        scatter_dimension=0,
        tiled=True,
    ).astype(jnp.float32)
    encoded = (packed.astype(jnp.float32) + attended).astype(jnp.bfloat16)
    return encoded.reshape(1, 1, tok_rows, model_width)


def solution(mesh):
    return jax.shard_map(
        on_device,
        mesh=mesh,
        in_specs=(
            P("dp", "mp", None, None),
            P("dp", "mp", None),
            P(),
            P(),
            P(),
            P(),
            P(None, None, "mp"),
            P("mp", None),
            P("dp", None, "mp", None),
            P("dp", "mp", None),
            P("dp", None, None),
        ),
        out_specs=P("dp", "mp", None, None),
        check_vma=False,
    )
```

profile of v0, /device:TPU:1, one launch (start us, length us, event | category | flops | bytes accessed | tf_op | source)
XLA Modules:
  0.0 175.0 jit_solution(10448039616900029444)
XLA Ops:
  6.6 0.8 broadcast_maximum_fusion
  7.4 0.7 compare_bitcast_fusion
  8.1 1.7 cosine_select_fusion
  9.8 0.1 fusion.31
  10.0 1.1 pad.9
  11.1 0.7 reshape.187
  11.8 1.2 fusion.56
  13.0 1.2 copy.37
  14.2 2.0 %copy.38 = bf16[4,256,160]{1,2,0:T(8,128)(2,1)} copy(bf16[4,256,160]{2,1,0:T(8,128)(2,1)} %get-tuple-element.8) | data formatting | bytes 655360
  16.2 0.9 copy.39
  17.1 1.9 %fusion.36 = f32[4,256,512]{2,1,0:T(8,128)S(1)} fusion(bf16[400,512]{1,0:T(8,128)(2,1)S(1)} %fusion.31, bf16[4,256,160]{1,2,0:T(8,128)(2,1)} %copy.39, bf16[4,256,160]{1,2,0:T(8,128)(2,1)} %copy.38, bf16[4,256,160]{1,2,0:T(8,128)(2,1)S(1)} %copy.37), kind=kOutput, calls=%fused_computation.58 | convolution fusion | flops 421888000 | bytes 3489792 | tf_op jit(solution)/shard_map/ufn,nk->ufk/dot_general | solution.py:68
  19.0 0.8 convolution_add_fusion
  20.2 1.2 fusion.20
  21.4 0.2 copy.40
  21.5 0.1 pad.10.clone
  21.7 0.2 fusion.44
  22.0 1.3 copy.25
  23.3 5.1 %fusion.8 = bf16[40,32,17,64]{3,1,2,0:T(8,128)(2,1)S(1)} fusion(pred[32,17]{0,1:T(8,128)(4,1)S(1)} %copy-done.9, bf16[1,80,32,36]{2,0,3,1:T(2,128)(2,1)S(1)} %copy.25, bf16[64,1,3,3]{0,3,2,1:T(4,128)(2,1)S(1)} %copy-done.6), kind=kOutput, calls=%fused_computation.16 | convolution fusion | flops 30429184 | bytes 2971296 | tf_op jit(solution)/shard_map/conv_general_dilated | solution.py:85
  28.4 2.2 %copy.27 = bf16[40,32,17,64]{3,0,2,1:T(8,128)(2,1)S(1)} copy(bf16[40,32,17,64]{3,1,2,0:T(8,128)(2,1)S(1)} %fusion.8) | data formatting | bytes 5570560 | tf_op jit(solution)/shard_map/convert_element_type | solution.py:93
  30.6 0.9 slice.63
  31.5 1.4 copy.28
  32.9 0.9 fusion.55
  33.8 4.8 %fusion.3 = bf16[40,4,8,18,64]{4,3,2,1,0:T(8,128)(2,1)S(1)} fusion(bf16[40,4,7,1,64]{4,3,2,1,0:T(2,128)(2,1)S(1)} %get-tuple-element.6, bf16[40,4,7,1,64]{4,3,2,1,0:T(2,128)(2,1)S(1)} %get-tuple-element.5, bf16[40,4,8,16,64]{4,3,2,1,0:T(8,128)(2,1)S(1)} %bitcast.88), kind=kLoop, calls=%fused_computation.8 | loop fusion | flops 14745600 | bytes 5857280 | tf_op jit(solution)/shard_map/convert_element_type | solution.py:93
  38.6 4.8 %maximum_convert_fusion.1 = bf16[20,32,8,64]{3,1,2,0:T(8,128)(2,1)S(1)} fusion(bf16[64,64,3,3]{1,0,3,2:T(8,128)(2,1)S(1)} %copy-done.5, bf16[40,4,8,18,64]{4,3,2,1,0:T(8,128)(2,1)S(1)} %fusion.3), kind=kOutput, calls=%fused_computation.24 | convolution fusion | flops 371851264 | bytes 3678208 | tf_op jit(solution)/shard_map/conv_general_dilated | solution.py:94
  43.4 0.6 copy.30
  44.0 2.6 %copy.31 = bf16[4,64,64,20]{1,0,3,2:T(4,128)(2,1)} copy(bf16[4,64,64,20]{2,1,0,3:T(8,128)(2,1)S(1)} %bitcast.90) | data formatting | bytes 1310720 | tf_op jit(solution)/shard_map/convert_element_type | solution.py:102
  46.6 2.3 %reshape.188 = bf16[256,1280]{0,1:T(8,128)(2,1)S(1)} reshape(bf16[4,64,64,20]{1,0,3,2:T(4,128)(2,1)} %copy.31) | data formatting | bytes 1310720 | tf_op jit(solution)/shard_map/reshape | solution.py:104
  49.1 3.3 %convolution_convert_fusion.2 = bf16[256,1536]{1,0:T(8,128)(2,1)S(1)} fusion(bf16[256,1280]{0,1:T(8,128)(2,1)S(1)} %reshape.188, bf16[1280,1536]{1,0:T(8,128)(2,1)} %param.15), kind=kOutput, calls=%fused_computation.25 | convolution fusion | flops 1007026176 | bytes 5373952 | tf_op jit(solution)/shard_map/dot_general | solution.py:151
  52.5 1.3 gather_fusion
  53.7 0.2 gather.11
  54.0 1.3 broadcast_select_fusion
  55.4 13.1 %all-to-all-start = ((bf16[64,4,1536]{2,1,0:T(4,128)(2,1)}), bf16[64,4,1536]{2,1,0:T(4,128)(2,1)S(1)}, u32[]{:S(2)}, u32[]{:S(2)}) async-start(bf16[64,4,1536]{2,1,0:T(4,128)(2,1)} %broadcast_select_fusion), calls=%async_computation | async-start | bytes 1572864 | tf_op jit(solution)/shard_map/all_to_all | solution.py:155
  68.6 22.9 %all-to-all-done = bf16[64,4,1536]{2,1,0:T(4,128)(2,1)S(1)} async-done(((bf16[64,4,1536]{2,1,0:T(4,128)(2,1)}), bf16[64,4,1536]{2,1,0:T(4,128)(2,1)S(1)}, u32[]{:S(2)}, u32[]{:S(2)}) %all-to-all-start) | async-done | bytes 786464 | tf_op jit(solution)/shard_map/all_to_all | solution.py:155
  91.5 0.2 reshape.189
  91.6 0.9 gather_fusion.1
  92.5 0.2 convert_reduce_fusion
  92.8 0.3 fusion.25
  93.1 1.3 fusion.27
  94.4 6.4 %copy.33 = bf16[1536,3,384]{0,2,1:T(8,128)(2,1)} copy(bf16[1536,3,384]{2,0,1:T(8,128)(2,1)} %param.17) | data formatting | bytes 7077888 | tf_op args[6]
  100.8 0.2 broadcast_compare_fusion
  101.0 19.6 %all-gather.2.cloned.1.call-done = bf16[512,1536]{1,0:T(8,128)(2,1)} async-done(((bf16[128,1536]{1,0:T(8,128)(2,1)}), bf16[512,1536]{1,0:T(8,128)(2,1)}) %all-gather.2.cloned.1.call-update) | async-done | bytes 1572880 | tf_op jit(solution)/shard_map/all_gather | solution.py:163
  120.6 5.7 %convolution_convert_fusion = bf16[512,1152]{1,0:T(8,128)(2,1)} fusion(bf16[512,1536]{1,0:T(8,128)(2,1)} %all-gather.2.cloned.1.call-done, bf16[1536,1152]{0,1:T(8,128)(2,1)} %bitcast.91), kind=kOutput, calls=%fused_computation.22 | convolution fusion | flops 1812529152 | bytes 6291456 | tf_op jit(solution)/shard_map/dot_general | solution.py:162
  126.4 1.6 copy.34
  128.0 5.1 %fusion.58 = (f32[6,512]{1,0:T(8,128)S(1)}, f32[6,512,512]{1,2,0:T(8,128)}) fusion(pred[512,512]{0,1:T(8,128)(4,1)S(1)} %broadcast_compare_fusion, bf16[512,3,6,64]{0,3,2,1:T(8,128)(2,1)S(1)} %bitcast.93), kind=kOutput, calls=%fused_computation.106 | convolution fusion | flops 207618560 | bytes 7352320 | tf_op jit(solution)/shard_map/sub | solution.py:121
  133.0 3.5 %fusion.16 = bf16[6,64,512]{2,1,0:T(8,128)(2,1)S(1)} fusion(f32[6,512,512]{1,2,0:T(8,128)} %get-tuple-element.17, f32[6,512]{1,0:T(8,128)S(1)} %get-tuple-element.16, bf16[512,3,6,64]{0,3,2,1:T(8,128)(2,1)S(1)} %bitcast.94), kind=kOutput, calls=%fused_computation.27 | convolution fusion | flops 204668928 | bytes 7094272 | tf_op jit(solution)/shard_map/hqk,khd->qhd/dot_general | solution.py:123
  136.5 2.2 %convolution_convert_fusion.1 = bf16[512,1536]{1,0:T(8,128)(2,1)} fusion(bf16[512,384]{0,1:T(8,128)(2,1)S(1)} %bitcast.97, bf16[384,1536]{1,0:T(8,128)(2,1)S(1)} %copy-done), kind=kOutput, calls=%fused_computation.23 | convolution fusion | flops 604766208 | bytes 3145728 | tf_op jit(solution)/shard_map/dot_general | solution.py:173
  138.7 27.6 %reduce-scatter.2.cloned.1.call-done = bf16[128,1536]{1,0:T(8,128)(2,1)} async-done(((bf16[512,1536]{1,0:T(8,128)(2,1)}), bf16[128,1536]{1,0:T(8,128)(2,1)}) %reduce-scatter.2.cloned.1.call-update) | async-done | bytes 393232 | tf_op jit(solution)/shard_map/reduce_scatter | solution.py:172
  166.3 1.9 %fusion.42 = bf16[1,1,128,1536]{3,2,1,0:T(8,128)(2,1)} fusion(bf16[128,1536]{1,0:T(8,128)(2,1)} %reduce-scatter.2.cloned.1.call-done, bf16[128,1536]{1,0:T(8,128)(2,1)S(1)} %gather_fusion.1, pred[128]{0:T(512)(128)(4,1)S(1)} %compare_and_fusion), kind=kLoop, calls=%fused_computation.67 | loop fusion | flops 983040 | bytes 1179776 | tf_op jit(solution)/shard_map/reshape | solution.py:179
  (43 shorter events, 1.0 us)
Async XLA Ops:
  6.5 130.0 %copy-start = (bf16[384,1536]{1,0:T(8,128)(2,1)S(1)}, bf16[384,1536]{1,0:T(8,128)(2,1)}, u32[]{:S(2)}) copy-start(bf16[384,1536]{1,0:T(8,128)(2,1)} %param.18) | copy-start | bytes 3538948
  17.1 1.9 %copy-start.1 = (bf16[4,256,160]{1,2,0:T(8,128)(2,1)S(1)}, bf16[4,256,160]{1,2,0:T(8,128)(2,1)}, u32[]{:S(2)}) copy-start(bf16[4,256,160]{1,2,0:T(8,128)(2,1)} %copy.38) | copy-start | bytes 983044
  17.1 1.9 %copy-start.2 = (bf16[4,256,160]{1,2,0:T(8,128)(2,1)S(1)}, bf16[4,256,160]{1,2,0:T(8,128)(2,1)}, u32[]{:S(2)}) copy-start(bf16[4,256,160]{1,2,0:T(8,128)(2,1)} %copy.39) | copy-start | bytes 983044
  19.0 0.9 copy-start.7
  19.9 3.4 %copy-start.6 = (bf16[64,1,3,3]{0,3,2,1:T(4,128)(2,1)S(1)}, bf16[64,1,3,3]{0,3,2,1:T(4,128)(2,1)}, u32[]{:S(2)}) copy-start(bf16[64,1,3,3]{0,3,2,1:T(4,128)(2,1)} %param.13) | copy-start | bytes 3460
  19.9 3.4 %copy-start.9 = (pred[32,17]{0,1:T(8,128)(4,1)S(1)}, pred[32,17]{0,1:T(8,128)(4,1)}, u32[]{:S(2)}) copy-start(pred[32,17]{0,1:T(8,128)(4,1)} %constant.109) | copy-start | bytes 1636
  33.8 4.8 %copy-start.5 = (bf16[64,64,3,3]{1,0,3,2:T(8,128)(2,1)S(1)}, bf16[64,64,3,3]{1,0,3,2:T(8,128)(2,1)}, u32[]{:S(2)}) copy-start(bf16[64,64,3,3]{1,0,3,2:T(8,128)(2,1)} %param.14) | copy-start | bytes 221188
  53.7 14.8 %copy-start.8 = (s32[1,1,128]{2,1,0:T(1,128)S(1)}, s32[1,1,128]{2,1,0:T(1,128)}, u32[]{:S(2)}) copy-start(s32[1,1,128]{2,1,0:T(1,128)} %param.20) | copy-start | bytes 1540
  55.4 37.7 %copy-start.3 = (f32[1536]{0:T(1024)S(1)}, f32[1536]{0:T(1024)}, u32[]{:S(2)}) copy-start(f32[1536]{0:T(1024)} %param.16) | copy-start | bytes 18436
  55.4 36.1 %all-to-all-start = ((bf16[64,4,1536]{2,1,0:T(4,128)(2,1)}), bf16[64,4,1536]{2,1,0:T(4,128)(2,1)S(1)}, u32[]{:S(2)}, u32[]{:S(2)}) async-start(bf16[64,4,1536]{2,1,0:T(4,128)(2,1)} %broadcast_select_fusion), calls=%async_computation | async-start | bytes 1572864 | tf_op jit(solution)/shard_map/all_to_all | solution.py:155
  68.5 52.2 %all-gather.2.cloned.1.call-start = ((), (), s32[]{:S(2)}) async-start(), calls=%async_computation.2 | async-start | bytes 1966080 | tf_op jit(solution)/shard_map/all_gather | solution.py:163
  94.4 6.4 %copy-start.4 = (s32[1,4,128]{2,1,0:T(4,128)S(1)}, s32[1,4,128]{2,1,0:T(4,128)}, u32[]{:S(2)}) copy-start(s32[1,4,128]{2,1,0:T(4,128)} %param.21) | copy-start | bytes 6148
  94.4 71.9 %reduce-scatter.2.cloned.1.call-start = ((), (), s32[]{:S(2)}) async-start(), calls=%async_computation.3 | async-start | bytes 1966080 | tf_op jit(solution)/shard_map/reduce_scatter | solution.py:172
Sparse Core Ops, SparseCore 0:
  94.5 26.1 all-gather.1
  138.8 27.4 reduce-scatter.1
where the time goes:
time: 176 us; the launch traced here: 175 us
  waiting for transfers between devices  70.1 us (40%)
  matrix products  33.5 us (19%)
  local copies, waits for them, and re-layouts  30.5 us (17%)
  other arithmetic  13.9 us (8%)
  between operations  13.8 us (8%)
  starting transfers between devices  13.2 us (8%)
    reduce_scatter x1, waiting for transfers between devices, on_device(): lax.psum_scatter(jnp.dot(contexts, attention_out, preferred_element_type=...  27.6 us
    all_to_all x1, waiting for transfers between devices, on_device(): lax.all_to_all(outgoing, 'dp', split_axis=0, concat_axis=0, tiled=True)  22.9 us
    all_gather x1, waiting for transfers between devices, on_device(): lax.all_gather(normed, 'mp', axis=0, tiled=True)  19.6 us
    all_to_all x1, starting transfers between devices, on_device(): lax.all_to_all(outgoing, 'dp', split_axis=0, concat_axis=0, tiled=True)  13.1 us
    unnamed x25, local copies, waits for them, and re-layouts  10.7 us
    dot_general x1, matrix products, on_device(): jnp.dot(lax.all_gather(normed, 'mp', axis=0, tiled=True), projector, pref...  5.74 us
    convert_element_type x4, local copies, waits for them, and re-layouts, subsample(): hidden = jnp.maximum(hidden, 0.0).astype(jnp.bfloat16)  5.32 us
    conv_general_dilated x1, matrix products, subsample(): lax.conv_general_dilated(log_image[:, None], conv_first, (2, 2), ((1, 1),...  5.12 us
  transfers between devices with their start and end apart: 3, of which 3 were waited for; matrix products, arithmetic and copies ran while one was open for 4% of the time, Pallas kernels for 0%

commit v1 on v0

v1 whole, which is shorter than its diff:
```python
import functools
import math

import jax
import jax.numpy as jnp
import ml_dtypes
import numpy as np
from jax import lax
from jax.experimental import pallas as pl
from jax.experimental.pallas import tpu as pltpu
from jax.sharding import PartitionSpec as P

N_MEL = 80
N_FFT = 400
HOP = 160
HEAD_DIM = 64
SLOT_ROWS = 64
CH = 64
MEL_HALF = 40
MEL_SUB = 20
STEP = 4 * HOP
ROW = 4 * N_MEL
WINDOW = 2 * ROW
MESH = pl.DeviceIdType.MESH
VMEM = pltpu.VMEM
BF16 = jnp.bfloat16
F32 = jnp.float32


def split_table(table):
    high = table.astype(ml_dtypes.bfloat16)
    low = (table - high.astype(np.float64)).astype(ml_dtypes.bfloat16)
    return high, low


def dft_tables():
    position = np.arange(N_FFT)[:, None]
    harmonic = np.arange(256)[None, :]
    angles = 2.0 * math.pi * ((position * harmonic) % N_FFT) / N_FFT
    window = (0.5 - 0.5 * np.cos(2.0 * math.pi * position / N_FFT)) / math.sqrt(N_FFT)
    inside = harmonic <= N_FFT // 2
    base = np.concatenate(
        [np.where(inside, np.cos(angles), 0.0), np.where(inside, -np.sin(angles), 0.0)], axis=1
    )
    table = np.zeros((4, 512, 512))
    for r in range(4):
        table[r, 32 * r : 32 * r + N_FFT] = base * window
    return split_table(table)


def mel_tables():
    frequency = np.arange(N_FFT // 2 + 1) * (16000.0 / N_FFT)
    mel_top = 2595.0 * math.log10(1.0 + 8000.0 / 700.0)
    points = np.arange(N_MEL + 2) * (mel_top / (N_MEL + 1))
    hertz = 700.0 * (10.0 ** (points / 2595.0) - 1.0)
    lower, centre, upper = hertz[:-2], hertz[1:-1], hertz[2:]
    rising = (frequency[:, None] - lower) / (centre - lower)
    falling = (upper - frequency[:, None]) / (upper - centre)
    weights = np.maximum(0.0, np.minimum(rising, falling))
    table = np.zeros((4, 256, WINDOW))
    for r in range(4):
        for half in range(2):
            start = half * ROW + r * N_MEL
            table[r, : N_FFT // 2 + 1, start : start + N_MEL] = weights
    return split_table(table)


def dot(a, b):
    return jnp.dot(a, b, preferred_element_type=F32)


def frontend_kernel(x, dft_high, dft_low, mel_high, mel_low, lengths, picks, out):
    rows = x.shape[0]
    energy = jnp.zeros((rows, WINDOW), F32)
    for r in range(4):
        samples = x[:, 128 * r : 128 * r + 512]
        spectrum = dot(samples, dft_high[r]) + dot(samples, dft_low[r])
        power = spectrum[:, :256] * spectrum[:, :256] + spectrum[:, 256:] * spectrum[:, 256:]
        high = power.astype(BF16)
        low = (power - high.astype(F32)).astype(BF16)
        energy += dot(high, mel_high[r]) + dot(low, mel_high[r]) + dot(high, mel_low[r])
    row = lax.broadcasted_iota(jnp.int32, (rows, 1), 0)
    limit = jnp.full((rows, 1), lengths[0], jnp.int32)
    for u in range(1, rows // SLOT_ROWS):
        limit = jnp.where(row >= u * SLOT_ROWS, lengths[u], limit)
    audible = row % SLOT_ROWS < limit
    image = jnp.where(audible, jnp.log(energy + 0.01), 0.0).astype(BF16)
    pick = picks[...]
    before = jnp.where(pick % SLOT_ROWS == 0, -1, pick - 1)
    column = lax.broadcasted_iota(jnp.int32, (pick.shape[0], rows), 1)
    take_own = (column == pick).astype(F32).astype(BF16)
    take_before = (column == before).astype(F32).astype(BF16)
    own = dot(take_own, image)
    earlier = dot(take_before, image)
    lane = lax.broadcasted_iota(jnp.int32, own.shape, 1)
    out[...] = jnp.where(lane < ROW, earlier, own).astype(BF16)


def exchange_kernel(count, x, out, send_sems, recv_sems, local_sem):
    me, lane = lax.axis_index("dp"), lax.axis_index("mp")
    barrier = pltpu.get_barrier_semaphore()

    @pl.loop(1, count)
    def _(d):
        pl.semaphore_signal(
            barrier, inc=1, device_id=(lax.rem(me + d, count), lane), device_id_type=MESH
        )

    own = pltpu.make_async_copy(x.at[me], out.at[me], local_sem)
    own.start()
    pl.semaphore_wait(barrier, count - 1)

    def copy_to(d):
        peer = lax.rem(me + d, count)
        return pltpu.make_async_remote_copy(
            src_ref=x.at[peer],
            dst_ref=out.at[me],
            send_sem=send_sems.at[d],
            recv_sem=recv_sems.at[d],
            device_id=(peer, lane),
            device_id_type=MESH,
        )

    @pl.loop(1, count)
    def _(d):
        copy_to(d).start()

    own.wait()

    @pl.loop(1, count)
    def _(d):
        source = lax.rem(me + count - d, count)
        pltpu.make_async_remote_copy(
            src_ref=x.at[source],
            dst_ref=out.at[source],
            send_sem=send_sems.at[d],
            recv_sem=recv_sems.at[d],
            device_id=(source, lane),
            device_id_type=MESH,
        ).wait_recv()

    @pl.loop(1, count)
    def _(d):
        copy_to(d).wait_send()


def group_barrier(me, dp, count):
    barrier = pltpu.get_barrier_semaphore()
    for d in range(1, count):
        pl.semaphore_signal(
            barrier, inc=1, device_id=(dp, lax.rem(me + d, count)), device_id_type=MESH
        )
    return barrier


def gather_kernel(count, received, arrivals, out, send_sems, recv_sems):
    dp, me = lax.axis_index("dp"), lax.axis_index("mp")
    barrier = group_barrier(me, dp, count)
    arrival = arrivals[...]
    column = lax.broadcasted_iota(jnp.int32, (arrival.shape[0], received.shape[0]), 1)
    take = (column == arrival).astype(F32).astype(BF16)
    out[0] = dot(take, received[...]).astype(BF16)
    pl.semaphore_wait(barrier, count - 1)
    copies = []
    for d in range(1, count):
        copy = pltpu.make_async_remote_copy(
            src_ref=out.at[0],
            dst_ref=out.at[count - d],
            send_sem=send_sems.at[d],
            recv_sem=recv_sems.at[count - d],
            device_id=(dp, lax.rem(me + d, count)),
            device_id_type=MESH,
        )
        copy.start()
        copies.append(copy)
    for d in range(1, count):
        pltpu.make_async_remote_copy(
            src_ref=out.at[0],
            dst_ref=out.at[d],
            send_sem=send_sems.at[d],
            recv_sem=recv_sems.at[d],
            device_id=(dp, lax.rem(me + d, count)),
            device_id_type=MESH,
        ).wait_recv()
    for copy in copies:
        copy.wait_send()


def context_kernel(count, x, out, send_sems, recv_sems, local_sem):
    dp, me = lax.axis_index("dp"), lax.axis_index("mp")
    barrier = group_barrier(me, dp, count)
    own = pltpu.make_async_copy(x.at[0], out.at[me], local_sem)
    own.start()
    pl.semaphore_wait(barrier, count - 1)
    copies = []
    for d in range(1, count):
        copy = pltpu.make_async_remote_copy(
            src_ref=x.at[d],
            dst_ref=out.at[me],
            send_sem=send_sems.at[d],
            recv_sem=recv_sems.at[count - d],
            device_id=(dp, lax.rem(me + d, count)),
            device_id_type=MESH,
        )
        copy.start()
        copies.append(copy)
    own.wait()
    for d in range(1, count):
        source = lax.rem(me + d, count)
        pltpu.make_async_remote_copy(
            src_ref=x.at[d],
            dst_ref=out.at[source],
            send_sem=send_sems.at[d],
            recv_sem=recv_sems.at[d],
            device_id=(dp, source),
            device_id_type=MESH,
        ).wait_recv()
    for copy in copies:
        copy.wait_send()


def tables_kernel(first, second, first_table, second_table):
    mel = lax.broadcasted_iota(jnp.int32, (N_MEL, MEL_HALF * CH), 0)
    band = lax.broadcasted_iota(jnp.int32, (N_MEL, MEL_HALF * CH), 1) // CH
    offset = mel - 2 * band + 1
    for t in range(3):
        rows = jnp.zeros(offset.shape, F32)
        for d in range(3):
            rows = jnp.where(offset == d, first[3 * t + d : 3 * t + d + 1, :], rows)
        first_table[t * N_MEL : (t + 1) * N_MEL, :] = rows.astype(BF16)
    first_table[3 * N_MEL :, :] = jnp.zeros((256 - 3 * N_MEL, MEL_HALF * CH), BF16)
    spread_row = lax.broadcasted_iota(jnp.int32, (CH, 4 * CH), 0)
    spread_column = lax.broadcasted_iota(jnp.int32, (CH, 4 * CH), 1)
    spread = (spread_row == spread_column // 4).astype(F32).astype(BF16)
    sub_band = lax.broadcasted_iota(jnp.int32, (CH, 4 * CH), 1) % 4
    for t in range(3):
        wide = [
            dot(second[(3 * t + d) * CH : (3 * t + d + 1) * CH, :], spread) for d in range(3)
        ]
        for k in range(10):
            block = jnp.zeros((CH, 4 * CH), F32)
            for d in range(3):
                block = jnp.where(2 * sub_band + d + 1 == k, wide[d], block)
            second_table[t, k * CH : (k + 1) * CH, :] = block.astype(BF16)


def block_kernel(
    windows,
    first_table,
    second_table,
    input_weight,
    norm_gain,
    attention_in,
    ids_row,
    ids_column,
    contexts,
    own_rows,
    shifted,
    hidden,
    features,
    embedded,
    normed,
    projected,
):
    blocks, per_block = windows.shape[0], windows.shape[1]
    rows = blocks * per_block
    width = MEL_HALF * CH
    model = input_weight.shape[1]
    shifted[:, :, 3 * N_MEL :] = jnp.zeros((3, rows, 256 - 3 * N_MEL), BF16)
    hidden[:, :, :128] = jnp.zeros((3, rows, 128), BF16)
    image = windows[...].reshape(rows, WINDOW)
    for t in range(3):
        start = (1 + 2 * t) * N_MEL
        shifted[t, :, : 3 * N_MEL] = image[:, start : start + 3 * N_MEL]
    for t in range(3):
        for n in range(width // 256):
            value = dot(shifted[t], first_table[:, n * 256 : (n + 1) * 256])
            hidden[t, :, 128 + n * 256 : 128 + (n + 1) * 256] = jnp.maximum(value, 0.0).astype(BF16)
    for g in range(5):
        value = dot(hidden[0, :, 512 * g : 512 * g + 640], second_table[0])
        value += dot(hidden[1, :, 512 * g : 512 * g + 640], second_table[1])
        value += dot(hidden[2, :, 512 * g : 512 * g + 640], second_table[2])
        features[:, 256 * g : 256 * (g + 1)] = jnp.maximum(value, 0.0).astype(BF16)
    for n in range(model // 256):
        embedded[:, n * 256 : (n + 1) * 256] = dot(
            features[...], input_weight[:, n * 256 : (n + 1) * 256]
        ).astype(BF16)
    own_rows[...] = embedded[:per_block, :]
    for b in range(blocks):
        values = embedded[b * per_block : (b + 1) * per_block, :].astype(F32)
        centre = values - jnp.mean(values, axis=-1, keepdims=True)
        spread = jnp.mean(centre * centre, axis=-1, keepdims=True)
        normed[b * per_block : (b + 1) * per_block, :] = (
            centre * lax.rsqrt(spread + 1e-05) * norm_gain[...]
        ).astype(BF16)
    local = attention_in.shape[2]
    for part in range(3):
        projected[part] = dot(normed[...], attention_in[part]).astype(BF16)
    lane = lax.broadcasted_iota(jnp.int32, (per_block, 128), 1)
    lower = lane < HEAD_DIM
    zero = jnp.zeros((per_block, 128), BF16)
    for b in range(blocks):
        same = ids_column[b] == ids_row[b]
        span = slice(b * per_block, (b + 1) * per_block)
        for pair in range(local // 128):
            lanes = slice(pair * 128, (pair + 1) * 128)
            query = projected[0, span, lanes]
            key = projected[1, span, lanes]
            value = projected[2, span, lanes]
            key_pair = jnp.concatenate(
                [jnp.where(lower, key, zero), jnp.where(lower, zero, key)], axis=0
            )
            value_pair = jnp.concatenate(
                [jnp.where(lower, value, zero), jnp.where(lower, zero, value)], axis=0
            )
            scores = lax.dot_general(
                query, key_pair, (((1,), (1,)), ((), ())), preferred_element_type=F32
            ) * (1.0 / math.sqrt(HEAD_DIM))
            weights = []
            for half in range(2):
                part = jnp.where(same, scores[:, half * per_block : (half + 1) * per_block], -jnp.inf)
                largest = jnp.max(part, axis=-1, keepdims=True)
                exponent = jnp.exp(part - largest)
                total = jnp.sum(exponent, axis=-1, keepdims=True)
                weights.append((exponent / total).astype(BF16))
            contexts[b, :, lanes] = dot(jnp.concatenate(weights, axis=1), value_pair).astype(BF16)


def output_kernel(contexts, weight, residual, out):
    share = contexts.shape[2]
    total = residual[...].astype(F32)
    for m in range(contexts.shape[0]):
        total += dot(contexts[m], weight[m * share : (m + 1) * share, :])
    out[...] = total.astype(BF16)


def in_vmem(count):
    return [pl.BlockSpec(memory_space=VMEM)] * count


def shape_of(shape, dtype=BF16):
    return jax.ShapeDtypeStruct(shape, dtype)


def params(limit=48, **more):
    return pltpu.CompilerParams(vmem_limit_bytes=limit * 2**20, **more)


def on_device(
    dp_count,
    mp_count,
    waveform,
    lengths,
    conv_first,
    conv_second,
    input_weight,
    norm_gain,
    attention_in,
    attention_out,
    send_slots,
    receive_slots,
    segment_ids,
):
    signal = waveform[0, 0]
    utterances = signal.shape[0]
    capacity = send_slots.shape[3]
    slots = dp_count * capacity
    per_block = receive_slots.shape[2]
    model = input_weight.shape[1]
    local = attention_in.shape[2]
    whole_out = lax.all_gather(attention_out, "mp", axis=0, tiled=True)

    covered = SLOT_ROWS * STEP
    main = signal[:, :covered].reshape(utterances, SLOT_ROWS, STEP)
    following = jnp.concatenate(
        [main[:, 1:, :256], signal[:, None, covered : covered + 256]], axis=1
    )
    samples = jnp.concatenate([main, following], axis=2).reshape(utterances * SLOT_ROWS, 896)
    dft_high, dft_low = dft_tables()
    mel_high, mel_low = mel_tables()
    outgoing = pl.pallas_call(
        frontend_kernel,
        out_shape=shape_of((slots, WINDOW)),
        in_specs=in_vmem(5) + [pl.BlockSpec(memory_space=pltpu.SMEM)] + in_vmem(1),
        out_specs=pl.BlockSpec(memory_space=VMEM),
        compiler_params=params(),
        name="frontend",
    )(
        samples,
        jnp.asarray(dft_high),
        jnp.asarray(dft_low),
        jnp.asarray(mel_high),
        jnp.asarray(mel_low),
        lengths[0, 0],
        send_slots[0, :, 0, :].reshape(slots, 1),
    )

    received = pl.pallas_call(
        functools.partial(exchange_kernel, dp_count),
        out_shape=shape_of((dp_count, capacity, WINDOW)),
        in_specs=in_vmem(1),
        out_specs=pl.BlockSpec(memory_space=VMEM),
        scratch_shapes=[
            pltpu.SemaphoreType.DMA((dp_count,)),
            pltpu.SemaphoreType.DMA((dp_count,)),
            pltpu.SemaphoreType.DMA,
        ],
        compiler_params=params(collective_id=0, has_side_effects=True),
        name="exchange",
    )(outgoing.reshape(dp_count, capacity, WINDOW))

    windows = pl.pallas_call(
        functools.partial(gather_kernel, mp_count),
        out_shape=shape_of((mp_count, per_block, WINDOW)),
        in_specs=in_vmem(2),
        out_specs=pl.BlockSpec(memory_space=VMEM),
        scratch_shapes=[
            pltpu.SemaphoreType.DMA((mp_count,)),
            pltpu.SemaphoreType.DMA((mp_count,)),
        ],
        compiler_params=params(collective_id=1, has_side_effects=True),
        name="gather",
    )(received.reshape(slots, WINDOW), receive_slots[0, 0].reshape(per_block, 1))

    first = conv_first.reshape(CH, 3, 3).transpose(2, 1, 0).reshape(9, CH).astype(F32)
    second = conv_second.transpose(3, 2, 1, 0).reshape(9 * CH, CH)
    first_table, second_table = pl.pallas_call(
        tables_kernel,
        out_shape=(shape_of((256, MEL_HALF * CH)), shape_of((3, 10 * CH, 4 * CH))),
        in_specs=in_vmem(2),
        out_specs=tuple(in_vmem(2)),
        compiler_params=params(),
        name="tables",
    )(jnp.tile(first, (1, MEL_HALF)), second)
    ordered_weight = (
        input_weight.reshape(CH, 5, 4, model).transpose(1, 0, 2, 3).reshape(CH * MEL_SUB, model)
    )
    me = lax.axis_index("mp")
    own_ids = jnp.roll(segment_ids[0], -me, axis=0)
    rows = mp_count * per_block
    contexts, own_rows = pl.pallas_call(
        block_kernel,
        out_shape=(shape_of((mp_count, per_block, local)), shape_of((per_block, model))),
        in_specs=in_vmem(8),
        out_specs=tuple(in_vmem(2)),
        scratch_shapes=[
            VMEM((3, rows, 256), BF16),
            VMEM((3, rows, 128 + MEL_HALF * CH), BF16),
            VMEM((rows, CH * MEL_SUB), BF16),
            VMEM((rows, model), BF16),
            VMEM((rows, model), BF16),
            VMEM((3, rows, local), BF16),
        ],
        compiler_params=params(),
        name="block",
    )(
        windows,
        first_table,
        second_table,
        ordered_weight,
        norm_gain.reshape(1, model),
        attention_in.transpose(1, 0, 2),
        own_ids.reshape(mp_count, 1, per_block),
        own_ids.reshape(mp_count, per_block, 1),
    )

    whole_contexts = pl.pallas_call(
        functools.partial(context_kernel, mp_count),
        out_shape=shape_of((mp_count, per_block, local)),
        in_specs=in_vmem(1),
        out_specs=pl.BlockSpec(memory_space=VMEM),
        scratch_shapes=[
            pltpu.SemaphoreType.DMA((mp_count,)),
            pltpu.SemaphoreType.DMA((mp_count,)),
            pltpu.SemaphoreType.DMA,
        ],
        compiler_params=params(collective_id=2, has_side_effects=True),
        name="contexts",
    )(contexts)

    encoded = pl.pallas_call(
        output_kernel,
        out_shape=shape_of((per_block, model)),
        in_specs=in_vmem(3),
        out_specs=pl.BlockSpec(memory_space=VMEM),
        compiler_params=params(),
        name="output",
    )(whole_contexts, whole_out, own_rows)
    return encoded.reshape(1, 1, per_block, model)


def solution(mesh):
    return jax.shard_map(
        functools.partial(on_device, mesh.shape["dp"], mesh.shape["mp"]),
        mesh=mesh,
        in_specs=(
            P("dp", "mp", None, None),
            P("dp", "mp", None),
            P(),
            P(),
            P(),
            P(),
            P(None, None, "mp"),
            P("mp", None),
            P("dp", None, "mp", None),
            P("dp", "mp", None),
            P("dp", None, None),
        ),
        out_specs=P("dp", "mp", None, None),
        check_vma=False,
    )
```

time: 176 us -> 112 us (0.64)
  waiting for transfers between devices: 70.1 us -> 0.73 us
  Pallas kernels: 0 us -> 67.8 us
  matrix products: 33.5 us -> 0 us
  other arithmetic: 13.9 us -> 0.07 us
  starting transfers between devices: 13.2 us -> 0.01 us
    pallas_call x0 -> x7, Pallas kernels: none -> 67.8 us  [the longest x1 22.1 us: on_device(): pl.pallas_call(functools.partial(exchange_kernel, dp_count), out_shape=sh...]
    reduce_scatter x1 -> x0, waiting for transfers between devices: 27.6 us -> none  [on_device(): lax.psum_scatter(jnp.dot(contexts, attention_out, preferred_element_type=...]
    all_to_all x1 -> x0, waiting for transfers between devices: 22.9 us -> none  [on_device(): lax.all_to_all(outgoing, 'dp', split_axis=0, concat_axis=0, tiled=True)]
    all_gather x1, waiting for transfers between devices: 19.6 us -> 0.02 us  [on_device(): whole_out = lax.all_gather(attention_out, 'mp', axis=0, tiled=True)]
    dot_general x7 -> x0, matrix products: 18.5 us -> none  [the longest x1 5.74 us: on_device(): jnp.dot(lax.all_gather(normed, 'mp', axis=0, tiled=True), projector, pref...]
    reshape x3 -> x8, local copies, waits for them, and re-layouts: 3.19 us -> 20.5 us  [the longest x3 20.2 us: on_device(): input_weight.reshape(CH, 5, 4, model).transpose(1, 0, 2, 3)]
    all_to_all x1 -> x0, starting transfers between devices: 13.1 us -> none  [on_device(): lax.all_to_all(outgoing, 'dp', split_axis=0, concat_axis=0, tiled=True)]
    convert_element_type x7 -> x2, local copies, waits for them, and re-layouts: 10.1 us -> 0.01 us  [on_device(): conv_first.reshape(CH, 3, 3).transpose(2, 1, 0).reshape(9, CH).astype(F32)]
  transfers between devices with their start and end apart: 3 -> 1, of which waited for: 3 -> 0; matrix products, arithmetic and copies ran while one was open for 4% -> 22% of each run, Pallas kernels for 0% -> 60%
where the time goes in v1:
time: 112 us; the launch traced here: 111 us
  Pallas kernels  67.8 us (61%)
  local copies, waits for them, and re-layouts  28.8 us (26%)
  between operations  13.7 us (12%)
    pallas_call x1, Pallas kernels, on_device(): pl.pallas_call(functools.partial(exchange_kernel, dp_count), out_shape=sh...  22.1 us
    reshape x3, local copies, waits for them, and re-layouts, on_device(): input_weight.reshape(CH, 5, 4, model).transpose(1, 0, 2, 3)  20.2 us
    pallas_call x1, Pallas kernels, on_device(): pl.pallas_call(block_kernel, out_shape=(shape_of((mp_count, per_block, lo...  16.2 us
    pallas_call x1, Pallas kernels, on_device(): pl.pallas_call(functools.partial(gather_kernel, mp_count), out_shape=shap...  14.2 us
    pallas_call x1, Pallas kernels, on_device(): pl.pallas_call(functools.partial(context_kernel, mp_count), out_shape=sha...  7.25 us
    unnamed x22, local copies, waits for them, and re-layouts  5.79 us
    pallas_call x1, Pallas kernels, on_device(): pl.pallas_call(frontend_kernel, out_shape=shape_of((slots, WINDOW)), in_s...  4.89 us
  transfers between devices with their start and end apart: 1, of which 0 were waited for; matrix products, arithmetic and copies ran while one was open for 22% of the time, Pallas kernels for 60%

profile of v1, /device:TPU:1, one launch (start us, length us, event | category | flops | bytes accessed | tf_op | source)
XLA Modules:
  0.0 111.1 jit_solution(4898898175606838721)
XLA Ops:
  6.5 0.0 copy-start.1
  6.5 0.0 copy-start.4
  6.5 0.0 all-gather.2.cloned.1.call-start
  6.5 0.7 all-gather.2.cloned.1.call-update
  7.3 1.1 slice.12
  8.4 0.7 slice_bitcast_fusion
  9.1 0.2 concatenate.15
  9.4 0.8 copy.22
  10.2 0.1 reshape_squeeze.8.picks
  10.3 0.0 copy-done.1
  10.3 0.0 copy-done.4
  10.4 0.0 copy-start.2
  10.4 1.3 %copy-done.2 = bf16[4,256,640]{2,1,0:T(8,128)(2,1)S(1)} copy-done((bf16[4,256,640]{2,1,0:T(8,128)(2,1)S(1)}, bf16[4,256,640]{2,1,0:T(8,128)(2,1)}, u32[]{:S(2)}) %copy-start.2) | copy-done | bytes 1310744
  11.7 0.0 copy-start.3
  11.7 1.3 %copy-done.3 = bf16[4,256,640]{2,1,0:T(8,128)(2,1)S(1)} copy-done((bf16[4,256,640]{2,1,0:T(8,128)(2,1)S(1)}, bf16[4,256,640]{2,1,0:T(8,128)(2,1)}, u32[]{:S(2)}) %copy-start.3) | copy-done | bytes 1310744
  13.0 0.0 copy-start.9
  13.0 0.0 copy-start.7
  13.0 0.0 copy-start.5
  13.0 4.9 %frontend.1 = bf16[256,640]{1,0:T(8,128)(2,1)S(1)} custom-call(bf16[256,896]{1,0:T(8,128)(2,1)S(1)} %pad_maximum_fusion.x, bf16[4,512,512]{2,1,0:T(8,128)(2,1)S(1)} %copy-done.1, bf16[4,512,512]{2,1,0:T(8,128)(2,1)} %constant.35.clone.dft_low, bf16[4,256,640]{2,1,0:T(8,128)(2,1)S(1)} %copy-done.2, bf16[4,256,640]{2,1,0:T(8,128)(2,1)S(1)} %copy-done.3, ...), custom_call_target="tpu_custom_call" | custom-call | tf_op jit(solution)/shard_map/frontend/pallas_call | solution.py:381
  17.9 0.1 reshape.49.x
  18.0 22.1 %exchange.1 = bf16[64,4,640]{2,1,0:T(4,128)(2,1)S(1)} custom-call(bf16[64,4,640]{2,1,0:T(4,128)(2,1)S(1)} %reshape.49.x), custom_call_target="tpu_custom_call" | custom-call | tf_op jit(solution)/shard_map/exchange/pallas_call | solution.py:398
  40.1 0.1 reshape.50.received
  40.1 0.0 copy-done.9
  40.2 0.1 copy.24.arrivals
  40.3 0.0 copy-done.7
  40.3 0.1 tile.10.first
  40.4 0.0 copy-done.5
  40.4 0.1 copy.26
  40.6 7.5 %reshape.52 = bf16[64,5,4,1536]{3,2,1,0:T(4,128)(2,1)} reshape(bf16[1280,1536]{1,0:T(8,128)(2,1)} %param.19) | data formatting | bytes 7864320 | tf_op jit(solution)/shard_map/reshape | solution.py:436
  48.1 5.4 %copy.32 = bf16[64,5,4,1536]{3,2,0,1:T(4,128)(2,1)} copy(bf16[64,5,4,1536]{3,2,1,0:T(4,128)(2,1)} %reshape.52) | data formatting | bytes 7864320 | tf_op jit(solution)/shard_map/reshape | solution.py:436
  53.5 0.0 copy-start.6
  53.5 0.0 copy-start.8
  53.5 7.3 %reshape.53.input_weight = bf16[1280,1536]{1,0:T(8,128)(2,1)} reshape(bf16[5,64,4,1536]{3,2,1,0:T(4,128)(2,1)} %bitcast.33) | data formatting | bytes 7864320 | tf_op jit(solution)/shard_map/reshape | solution.py:436
  60.8 0.0 copy-done.6
  60.8 0.0 copy-done.8
  60.8 0.1 copy.28.ids_column
  61.0 14.2 %gather.1.windows = bf16[4,128,640]{2,1,0:T(8,128)(2,1)S(1)} custom-call(bf16[256,640]{1,0:T(8,128)(2,1)S(1)} %reshape.50.received, s32[128,1]{1,0:T(8,128)S(1)} %copy.24.arrivals), custom_call_target="tpu_custom_call" | custom-call | tf_op jit(solution)/shard_map/gather/pallas_call | solution.py:412
  75.2 1.5 %tables.1 = (bf16[256,2560]{1,0:T(8,128)(2,1)S(1)}, bf16[3,640,256]{2,1,0:T(8,128)(2,1)S(1)}) custom-call(f32[9,2560]{1,0:T(8,128)S(1)} %tile.10.first, bf16[576,64]{1,0:T(8,128)(2,1)S(1)} %bitcast.30), custom_call_target="tpu_custom_call" | custom-call | tf_op jit(solution)/shard_map/tables/pallas_call | solution.py:427
  76.8 16.2 %block.1 = (bf16[4,128,384]{2,1,0:T(8,128)(2,1)S(1)}, bf16[128,1536]{1,0:T(8,128)(2,1)S(1)}) custom-call(bf16[4,128,640]{2,1,0:T(8,128)(2,1)S(1)} %gather.1.windows, bf16[256,2560]{1,0:T(8,128)(2,1)S(1)} %get-tuple-element.9.first_table, bf16[3,640,256]{2,1,0:T(8,128)(2,1)S(1)} %get-tuple-element.10.second_table, bf16[1280,1536]{1,0:T(8,128)(2,1)} %reshape.53.input_weight, ...), custom_call_target="tpu_custom_call" | custom-call | tf_op jit(solution)/shard_map/block/pallas_call | solution.py:441
  92.9 7.2 %contexts.1 = bf16[4,128,384]{2,1,0:T(8,128)(2,1)S(1)} custom-call(bf16[4,128,384]{2,1,0:T(8,128)(2,1)S(1)} %get-tuple-element.11.x), custom_call_target="tpu_custom_call" | custom-call | tf_op jit(solution)/shard_map/contexts/pallas_call | solution.py:467
  100.2 0.0 all-gather.2.cloned.1.call-done.weight
  100.2 0.0 copy-start
  100.2 2.3 %copy-done = bf16[1536,1536]{1,0:T(8,128)(2,1)S(1)} copy-done((bf16[1536,1536]{1,0:T(8,128)(2,1)S(1)}, bf16[1536,1536]{1,0:T(8,128)(2,1)}, u32[]{:S(2)}) %copy-start) | copy-done | bytes 4718616
  102.5 1.7 %output.1 = bf16[128,1536]{1,0:T(8,128)(2,1)} custom-call(bf16[4,128,384]{2,1,0:T(8,128)(2,1)S(1)} %contexts.1, bf16[1536,1536]{1,0:T(8,128)(2,1)S(1)} %copy-done, bf16[128,1536]{1,0:T(8,128)(2,1)S(1)} %get-tuple-element.12.residual), custom_call_target="tpu_custom_call" | custom-call | tf_op jit(solution)/shard_map/output/pallas_call | solution.py:481
  (13 shorter events, 0.2 us)
Async XLA Ops:
  6.5 3.8 %copy-start.1 = (bf16[4,512,512]{2,1,0:T(8,128)(2,1)S(1)}, bf16[4,512,512]{2,1,0:T(8,128)(2,1)}, u32[]{:S(2)}) copy-start(bf16[4,512,512]{2,1,0:T(8,128)(2,1)} %constant.34.clone.dft_high) | copy-start | bytes 6291460
  6.5 3.8 %copy-start.4 = (s32[1,1,4]{2,1,0:T(1,128)S(1)}, s32[1,1,4]{2,1,0:T(1,128)}, u32[]{:S(2)}) copy-start(s32[1,1,4]{2,1,0:T(1,128)} %param.16) | copy-start | bytes 52
  6.5 93.7 %all-gather.2.cloned.1.call-start = ((), (), s32[]{:S(2)}) async-start(), calls=%async_computation | async-start | bytes 5898240 | tf_op jit(solution)/shard_map/all_gather | solution.py:371
  10.4 1.3 %copy-start.2 = (bf16[4,256,640]{2,1,0:T(8,128)(2,1)S(1)}, bf16[4,256,640]{2,1,0:T(8,128)(2,1)}, u32[]{:S(2)}) copy-start(bf16[4,256,640]{2,1,0:T(8,128)(2,1)} %constant.36.clone.mel_high) | copy-start | bytes 3932164
  11.7 1.3 %copy-start.3 = (bf16[4,256,640]{2,1,0:T(8,128)(2,1)S(1)}, bf16[4,256,640]{2,1,0:T(8,128)(2,1)}, u32[]{:S(2)}) copy-start(bf16[4,256,640]{2,1,0:T(8,128)(2,1)} %constant.37.clone.mel_low) | copy-start | bytes 3932164
  13.0 27.2 %copy-start.9 = (s32[1,1,128]{2,1,0:T(1,128)S(1)}, s32[1,1,128]{2,1,0:T(1,128)}, u32[]{:S(2)}) copy-start(s32[1,1,128]{2,1,0:T(1,128)} %param.24) | copy-start | bytes 1540
  13.0 27.3 %copy-start.7 = (bf16[64,1,3,3]{0,3,2,1:T(4,128)(2,1)S(1)}, bf16[64,1,3,3]{0,3,2,1:T(4,128)(2,1)}, u32[]{:S(2)}) copy-start(bf16[64,1,3,3]{0,3,2,1:T(4,128)(2,1)} %param.17) | copy-start | bytes 3460
  13.0 27.4 %copy-start.5 = (bf16[64,64,3,3]{1,0,3,2:T(8,128)(2,1)S(1)}, bf16[64,64,3,3]{1,0,3,2:T(8,128)(2,1)}, u32[]{:S(2)}) copy-start(bf16[64,64,3,3]{1,0,3,2:T(8,128)(2,1)} %param.18) | copy-start | bytes 221188
  53.5 7.3 %copy-start.6 = (f32[1536]{0:T(1024)S(1)}, f32[1536]{0:T(1024)}, u32[]{:S(2)}) copy-start(f32[1536]{0:T(1024)} %param.20) | copy-start | bytes 18436
  53.5 7.3 %copy-start.8 = (s32[1,4,128]{2,1,0:T(4,128)S(1)}, s32[1,4,128]{2,1,0:T(4,128)}, u32[]{:S(2)}) copy-start(s32[1,4,128]{2,1,0:T(4,128)} %param.25) | copy-start | bytes 6148
  100.2 2.3 %copy-start = (bf16[1536,1536]{1,0:T(8,128)(2,1)S(1)}, bf16[1536,1536]{1,0:T(8,128)(2,1)}, u32[]{:S(2)}) copy-start(bf16[1536,1536]{1,0:T(8,128)(2,1)} %all-gather.2.cloned.1.call-done.weight) | copy-start | bytes 14155780
Sparse Core Ops, SparseCore 0:
  9.2 60.6 all-gather.1

commit v2 on v0

v2 whole, which is shorter than its diff:
```python
import functools
import math

import jax
import jax.numpy as jnp
import ml_dtypes
import numpy as np
from jax import lax
from jax.experimental import pallas as pl
from jax.experimental.pallas import tpu as pltpu
from jax.sharding import PartitionSpec as P

N_MEL = 80
N_FFT = 400
HOP = 160
HEAD_DIM = 64
SLOT_ROWS = 64
CH = 64
MEL_HALF = 40
MEL_SUB = 20
STEP = 4 * HOP
ROW = 4 * N_MEL
WINDOW = 2 * ROW
MESH = pl.DeviceIdType.MESH
VMEM = pltpu.VMEM
BF16 = jnp.bfloat16
F32 = jnp.float32


def dft_table():
    position = np.arange(N_FFT)[:, None]
    harmonic = np.arange(256)[None, :]
    angles = 2.0 * math.pi * ((position * harmonic) % N_FFT) / N_FFT
    window = (0.5 - 0.5 * np.cos(2.0 * math.pi * position / N_FFT)) / math.sqrt(N_FFT)
    inside = harmonic <= N_FFT // 2
    base = np.concatenate(
        [np.where(inside, np.cos(angles), 0.0), np.where(inside, -np.sin(angles), 0.0)], axis=1
    )
    table = np.zeros((4, 512, 512))
    for r in range(4):
        table[r, 32 * r : 32 * r + N_FFT] = base * window
    return table.astype(ml_dtypes.bfloat16)


def mel_table():
    frequency = np.arange(N_FFT // 2 + 1) * (16000.0 / N_FFT)
    mel_top = 2595.0 * math.log10(1.0 + 8000.0 / 700.0)
    points = np.arange(N_MEL + 2) * (mel_top / (N_MEL + 1))
    hertz = 700.0 * (10.0 ** (points / 2595.0) - 1.0)
    lower, centre, upper = hertz[:-2], hertz[1:-1], hertz[2:]
    rising = (frequency[:, None] - lower) / (centre - lower)
    falling = (upper - frequency[:, None]) / (upper - centre)
    weights = np.maximum(0.0, np.minimum(rising, falling))
    table = np.zeros((4, 256, WINDOW))
    for r in range(4):
        for half in range(2):
            start = half * ROW + r * N_MEL
            table[r, : N_FFT // 2 + 1, start : start + N_MEL] = weights
    return table.astype(ml_dtypes.bfloat16)


def dot(a, b):
    return jnp.dot(a, b, preferred_element_type=F32)


def one_hot(condition):
    return condition.astype(F32).astype(BF16)


def iota(shape, dimension):
    return lax.broadcasted_iota(jnp.int32, shape, dimension)


def contract(a, b, dim_a, dim_b):
    return lax.dot_general(a, b, (((dim_a,), (dim_b,)), ((), ())), preferred_element_type=F32)


def frontend_kernel(
    count,
    wave,
    lengths,
    picks,
    arrivals,
    conv_first,
    conv_second,
    dft_hbm,
    mel_hbm,
    weight_hbm,
    attention_hbm,
    windows,
    first_table,
    second_table,
    weight,
    attention,
    dft,
    mel,
    raw,
    samples,
    rows,
    outgoing,
    incoming,
    send_sems,
    recv_sems,
    local_sems,
):
    me, lane = lax.axis_index("dp"), lax.axis_index("mp")
    capacity = picks.shape[0]
    utterances = wave.shape[0]
    frames = utterances * SLOT_ROWS
    barrier = pltpu.get_barrier_semaphore()

    @pl.loop(1, count)
    def _(d):
        pl.semaphore_signal(
            barrier, inc=1, device_id=(lax.rem(me + d, count), lane), device_id_type=MESH
        )

    load_dft = pltpu.make_async_copy(dft_hbm, dft, local_sems.at[0])
    load_mel = pltpu.make_async_copy(mel_hbm, mel, local_sems.at[1])
    load_weight = pltpu.make_async_copy(weight_hbm, raw, local_sems.at[2])
    load_attention = pltpu.make_async_copy(attention_hbm, attention, local_sems.at[3])
    load_dft.start()
    load_mel.start()
    load_weight.start()
    load_attention.start()

    for s in range(SLOT_ROWS):
        samples[utterances * s : utterances * (s + 1), :] = wave[:, STEP * s : STEP * s + 896]
    load_dft.wait()
    load_mel.wait()
    energy = jnp.zeros((frames, WINDOW), F32)
    for r in range(4):
        spectrum = dot(samples[:, 128 * r : 128 * r + 512], dft[r])
        power = spectrum[:, :256] * spectrum[:, :256] + spectrum[:, 256:] * spectrum[:, 256:]
        energy += dot(power.astype(BF16), mel[r])
    row = iota((frames, 1), 0)
    limit = jnp.full((frames, 1), lengths[0], jnp.int32)
    for u in range(1, utterances):
        limit = jnp.where(row % utterances == u, lengths[u], limit)
    image = jnp.where(row // utterances < limit, jnp.log(energy + 0.01), 0.0).astype(BF16)

    slots = count * capacity
    target = (me + iota((slots, count), 0) // capacity) % count
    chosen = contract(one_hot(iota((slots, count), 1) == target), picks[...].astype(F32).astype(BF16), 1, 1)
    chosen = jnp.where(
        iota((slots, capacity), 1) == iota((slots, capacity), 0) % capacity, chosen, 0.0
    )
    pick = jnp.sum(chosen, axis=1, keepdims=True).astype(jnp.int32)
    place = jnp.where(pick < 0, -SLOT_ROWS, pick % SLOT_ROWS * utterances + pick // SLOT_ROWS)
    column = iota((slots, frames), 1)
    own = dot(one_hot(column == place), image)
    earlier = dot(one_hot(column == place - utterances), image)
    rows[...] = jnp.where(iota(own.shape, 1) < ROW, earlier, own)
    for d in range(count):
        slab = rows[capacity * d : capacity * (d + 1), :].astype(BF16)
        if d == 0:
            incoming[0] = slab
        else:
            outgoing[d] = slab

    pl.semaphore_wait(barrier, count - 1)

    def copy_to(d):
        return pltpu.make_async_remote_copy(
            src_ref=outgoing.at[d],
            dst_ref=incoming.at[d],
            send_sem=send_sems.at[d],
            recv_sem=recv_sems.at[d],
            device_id=(lax.rem(me + d, count), lane),
            device_id_type=MESH,
        )

    @pl.loop(1, count)
    def _(d):
        copy_to(d).start()

    twice = one_hot(iota((CH, 2 * CH), 0) == iota((CH, 2 * CH), 1) % CH)
    taps = [dot(conv_first[d], twice) for d in range(3)]
    first_table[3 * N_MEL :, :] = jnp.zeros((256 - 3 * N_MEL, MEL_HALF * CH), BF16)
    offset = iota((N_MEL, 2 * CH), 0) - 2 * (iota((N_MEL, 2 * CH), 1) // CH) + 1
    for n in range(MEL_HALF // 2):
        for t in range(3):
            block = jnp.zeros(offset.shape, F32)
            for d in range(3):
                block = jnp.where(offset - 4 * n == d, taps[d][t : t + 1, :], block)
            first_table[t * N_MEL : (t + 1) * N_MEL, 2 * CH * n : 2 * CH * (n + 1)] = block.astype(BF16)
    spread = one_hot(iota((CH, 4 * CH), 0) == iota((CH, 4 * CH), 1) // 4)
    sub_band = iota((CH, 4 * CH), 1) % 4
    for t in range(3):
        wide = [contract(conv_second[d, t], spread, 0, 0) for d in range(3)]
        for k in range(10):
            block = jnp.zeros((CH, 4 * CH), F32)
            for d in range(3):
                block = jnp.where(2 * sub_band + d + 1 == k, wide[d], block)
            second_table[t, k * CH : (k + 1) * CH, :] = block.astype(BF16)
    span = 16 * MEL_SUB
    out_row, in_row = iota((span, span), 0), iota((span, span), 1)
    source = (out_row % 64 // 4) * MEL_SUB + out_row // 64 * 4 + out_row % 4
    order = one_hot(in_row == source)
    load_weight.wait()
    for block in range(4):
        value = dot(order, raw[block * span : (block + 1) * span, :]).astype(BF16)
        for g in range(5):
            weight[256 * g + 64 * block : 256 * g + 64 * (block + 1), :] = value[64 * g : 64 * (g + 1), :]
    load_attention.wait()

    arrival = arrivals[...]
    position = (me + count - arrival // capacity) % count * capacity + arrival % capacity
    take = (iota((slots, arrival.shape[1]), 0) == position).astype(F32)
    take = jnp.transpose(take).astype(BF16)

    @pl.loop(1, count)
    def _(d):
        copy_to(d).wait_recv()

    for d in range(count):
        rows[capacity * d : capacity * (d + 1), :] = incoming[d].astype(F32)
    windows[...] = dot(take, rows[...].astype(BF16)).astype(BF16)

    @pl.loop(1, count)
    def _(d):
        copy_to(d).wait_send()


def block_kernel(
    count,
    own_windows,
    first_table,
    second_table,
    weight,
    norm_gain,
    attention,
    ids,
    contexts,
    own_rows,
    windows,
    shifted,
    hidden,
    features,
    embedded,
    normed,
    projected,
    sending,
    gather_send,
    gather_recv,
    context_send,
    context_recv,
):
    dp, me = lax.axis_index("dp"), lax.axis_index("mp")
    per_block = own_windows.shape[0]
    rows = count * per_block
    width = MEL_HALF * CH
    model = weight.shape[1]
    local = attention.shape[2]
    barrier = pltpu.get_barrier_semaphore()
    for d in range(1, count):
        pl.semaphore_signal(
            barrier, inc=1, device_id=(dp, lax.rem(me + d, count)), device_id_type=MESH
        )

    def peer(d):
        return (dp, lax.rem(me + d, count))

    def gather_copy(d):
        return pltpu.make_async_remote_copy(
            src_ref=own_windows,
            dst_ref=windows.at[count - d],
            send_sem=gather_send.at[d],
            recv_sem=gather_recv.at[count - d],
            device_id=peer(d),
            device_id_type=MESH,
        )

    def gather_arrival(d):
        return pltpu.make_async_remote_copy(
            src_ref=own_windows,
            dst_ref=windows.at[d],
            send_sem=gather_send.at[d],
            recv_sem=gather_recv.at[d],
            device_id=peer(d),
            device_id_type=MESH,
        )

    def context_copy(d):
        return pltpu.make_async_remote_copy(
            src_ref=sending.at[d],
            dst_ref=contexts.at[me],
            send_sem=context_send.at[d],
            recv_sem=context_recv.at[count - d],
            device_id=peer(d),
            device_id_type=MESH,
        )

    def context_arrival(d):
        return pltpu.make_async_remote_copy(
            src_ref=sending.at[d],
            dst_ref=contexts.at[lax.rem(me + d, count)],
            send_sem=context_send.at[d],
            recv_sem=context_recv.at[d],
            device_id=peer(d),
            device_id_type=MESH,
        )

    lower = iota((per_block, 128), 1) < HEAD_DIM
    zero = jnp.zeros((per_block, 128), BF16)

    def project(start, stop, image):
        span = slice(start, stop)
        for t in range(3):
            first = (1 + 2 * t) * N_MEL
            shifted[t, span, : 3 * N_MEL] = image[:, first : first + 3 * N_MEL]
        for t in range(3):
            for n in range(width // 256):
                value = dot(shifted[t, span, :], first_table[:, n * 256 : (n + 1) * 256])
                hidden[t, span, 128 + n * 256 : 128 + (n + 1) * 256] = jnp.maximum(value, 0.0).astype(BF16)
        for g in range(5):
            value = dot(hidden[0, span, 512 * g : 512 * g + 640], second_table[0])
            value += dot(hidden[1, span, 512 * g : 512 * g + 640], second_table[1])
            value += dot(hidden[2, span, 512 * g : 512 * g + 640], second_table[2])
            features[span, 256 * g : 256 * (g + 1)] = jnp.maximum(value, 0.0).astype(BF16)
        for n in range(model // 256):
            embedded[span, n * 256 : (n + 1) * 256] = dot(
                features[span, :], weight[:, n * 256 : (n + 1) * 256]
            ).astype(BF16)
        for b in range(start, stop, per_block):
            values = embedded[b : b + per_block, :].astype(F32)
            centre = values - jnp.mean(values, axis=-1, keepdims=True)
            spread = jnp.mean(centre * centre, axis=-1, keepdims=True)
            normed[b : b + per_block, :] = (
                centre * lax.rsqrt(spread + 1e-05) * norm_gain[...]
            ).astype(BF16)
        for part in range(3):
            projected[part, span, :] = dot(normed[span, :], attention[part]).astype(BF16)

    def attend(b, store):
        block_ids = ids[pl.ds(lax.rem(me + b, count), 1), :]
        across = jnp.broadcast_to(block_ids, (per_block, per_block))
        same = across == jnp.transpose(across)
        span = slice(b * per_block, (b + 1) * per_block)
        for pair in range(local // 128):
            lanes = slice(pair * 128, (pair + 1) * 128)
            query = projected[0, span, lanes]
            key = projected[1, span, lanes]
            value = projected[2, span, lanes]
            key_pair = jnp.concatenate(
                [jnp.where(lower, key, zero), jnp.where(lower, zero, key)], axis=0
            )
            value_pair = jnp.concatenate(
                [jnp.where(lower, value, zero), jnp.where(lower, zero, value)], axis=0
            )
            scores = contract(query, key_pair, 1, 1) * (1.0 / math.sqrt(HEAD_DIM))
            weights = []
            for half in range(2):
                part = jnp.where(same, scores[:, half * per_block : (half + 1) * per_block], -jnp.inf)
                largest = jnp.max(part, axis=-1, keepdims=True)
                exponent = jnp.exp(part - largest)
                total = jnp.sum(exponent, axis=-1, keepdims=True)
                weights.append((exponent / total).astype(BF16))
            store(lanes, dot(jnp.concatenate(weights, axis=1), value_pair).astype(BF16))

    def store_own(lanes, value):
        contexts[me, :, lanes] = value

    shifted[:, :, 3 * N_MEL :] = jnp.zeros((3, rows, 256 - 3 * N_MEL), BF16)
    hidden[:, :, :128] = jnp.zeros((3, rows, 128), BF16)
    pl.semaphore_wait(barrier, count - 1)
    for d in range(1, count):
        gather_copy(d).start()
    project(0, per_block, own_windows[...])
    attend(0, store_own)
    own_rows[...] = embedded[:per_block, :]
    for d in range(1, count):
        gather_arrival(d).wait_recv()
    project(per_block, rows, windows[1:].reshape(rows - per_block, WINDOW))
    for d in range(1, count):

        def store_sending(lanes, value, d=d):
            sending[d, :, lanes] = value

        attend(d, store_sending)
        context_copy(d).start()
    for d in range(1, count):
        context_arrival(d).wait_recv()
    for d in range(1, count):
        gather_copy(d).wait_send()
        context_copy(d).wait_send()


def output_kernel(contexts, near, far, residual, out):
    core = lax.rem(lax.axis_index("dp"), 2)
    share = contexts.shape[2]
    half = near.shape[1]
    for index, part in ((core, near), (1 - core, far)):
        lanes = pl.ds(pl.multiple_of(index * half, 128), half)
        total = residual[:, lanes].astype(F32)
        for m in range(contexts.shape[0]):
            total += dot(contexts[m], part[m * share : (m + 1) * share, :])
        out[:, lanes] = total.astype(BF16)


def in_vmem(count):
    return [pl.BlockSpec(memory_space=VMEM)] * count


def in_any(count):
    return [pl.BlockSpec(memory_space=pl.ANY)] * count


def shape_of(shape, dtype=BF16):
    return jax.ShapeDtypeStruct(shape, dtype)


def params(limit=48, **more):
    return pltpu.CompilerParams(vmem_limit_bytes=limit * 2**20, **more)


def on_device(
    dp_count,
    mp_count,
    waveform,
    lengths,
    conv_first,
    conv_second,
    input_weight,
    norm_gain,
    attention_in,
    attention_out,
    send_slots,
    receive_slots,
    segment_ids,
):
    capacity = send_slots.shape[3]
    per_block = receive_slots.shape[2]
    model = input_weight.shape[1]
    local = attention_in.shape[2]
    half = model // 2
    rows = mp_count * per_block
    dma = pltpu.SemaphoreType.DMA

    core = lax.rem(lax.axis_index("dp"), 2)
    own_half = lax.dynamic_slice_in_dim(attention_out, core * half, half, axis=1)
    near = lax.all_gather(own_half, "mp", axis=0, tiled=True)
    far = lax.ppermute(near, "dp", [(i, i ^ 1) for i in range(dp_count)])

    windows, first_table, second_table, weight, attention = pl.pallas_call(
        functools.partial(frontend_kernel, dp_count),
        out_shape=(
            shape_of((per_block, WINDOW)),
            shape_of((256, MEL_HALF * CH)),
            shape_of((3, 10 * CH, 4 * CH)),
            shape_of((CH * MEL_SUB, model)),
            shape_of((3, model, local)),
        ),
        in_specs=in_vmem(1) + [pl.BlockSpec(memory_space=pltpu.SMEM)] + in_vmem(4) + in_any(4),
        out_specs=tuple(in_vmem(5)),
        scratch_shapes=[
            VMEM((4, 512, 512), BF16),
            VMEM((4, 256, WINDOW), BF16),
            VMEM((CH * MEL_SUB, model), BF16),
            VMEM((4 * SLOT_ROWS, 896), BF16),
            VMEM((dp_count * capacity, WINDOW), F32),
            VMEM((dp_count, capacity, WINDOW), BF16),
            VMEM((dp_count, capacity, WINDOW), BF16),
            dma((dp_count,)),
            dma((dp_count,)),
            dma((4,)),
        ],
        compiler_params=params(collective_id=0, has_side_effects=True),
        name="frontend",
    )(
        waveform[0, 0],
        lengths[0, 0],
        send_slots[0, :, 0, :].transpose(1, 0),
        receive_slots[0],
        conv_first.transpose(1, 2, 3, 0)[0],
        conv_second.transpose(2, 3, 0, 1),
        jnp.asarray(dft_table()),
        jnp.asarray(mel_table()),
        input_weight,
        attention_in.transpose(1, 0, 2),
    )

    contexts, own_rows = pl.pallas_call(
        functools.partial(block_kernel, mp_count),
        out_shape=(shape_of((mp_count, per_block, local)), shape_of((per_block, model))),
        in_specs=in_vmem(7),
        out_specs=tuple(in_vmem(2)),
        scratch_shapes=[
            VMEM((mp_count, per_block, WINDOW), BF16),
            VMEM((3, rows, 256), BF16),
            VMEM((3, rows, 128 + MEL_HALF * CH), BF16),
            VMEM((rows, CH * MEL_SUB), BF16),
            VMEM((rows, model), BF16),
            VMEM((rows, model), BF16),
            VMEM((3, rows, local), BF16),
            VMEM((mp_count, per_block, local), BF16),
            dma((mp_count,)),
            dma((mp_count,)),
            dma((mp_count,)),
            dma((mp_count,)),
        ],
        compiler_params=params(collective_id=1, has_side_effects=True),
        name="block",
    )(
        windows,
        first_table,
        second_table,
        weight,
        norm_gain.reshape(1, model),
        attention,
        segment_ids[0],
    )

    encoded = pl.pallas_call(
        output_kernel,
        out_shape=shape_of((per_block, model)),
        in_specs=in_vmem(4),
        out_specs=pl.BlockSpec(memory_space=VMEM),
        compiler_params=params(),
        name="output",
    )(contexts, near, far, own_rows)
    return encoded.reshape(1, 1, per_block, model)


def solution(mesh):
    return jax.shard_map(
        functools.partial(on_device, mesh.shape["dp"], mesh.shape["mp"]),
        mesh=mesh,
        in_specs=(
            P("dp", "mp", None, None),
            P("dp", "mp", None),
            P(),
            P(),
            P(),
            P(),
            P(None, None, "mp"),
            P("mp", None),
            P("dp", None, "mp", None),
            P("dp", "mp", None),
            P("dp", None, None),
        ),
        out_specs=P("dp", "mp", None, None),
        check_vma=False,
    )
```

time: 176 us -> 117 us (0.66)
  Pallas kernels: 0 us -> 54.1 us
  matrix products: 33.5 us -> 0 us
  waiting for transfers between devices: 70.1 us -> 39.9 us
  local copies, waits for them, and re-layouts: 30.5 us -> 7.39 us
  other arithmetic: 13.9 us -> 0 us
  starting transfers between devices: 13.2 us -> 0.68 us
    pallas_call x0 -> x3, Pallas kernels: none -> 54.1 us  [the longest x1 28.8 us: on_device(): pl.pallas_call(functools.partial(block_kernel, mp_count), out_shape=(shap...]
    reduce_scatter x1 -> x0, waiting for transfers between devices: 27.6 us -> none  [on_device(): lax.psum_scatter(jnp.dot(contexts, attention_out, preferred_element_type=...]
    all_to_all x1 -> x0, waiting for transfers between devices: 22.9 us -> none  [on_device(): lax.all_to_all(outgoing, 'dp', split_axis=0, concat_axis=0, tiled=True)]
    all_gather x1, waiting for transfers between devices: 19.6 us -> 39.9 us  [on_device(): near = lax.all_gather(own_half, 'mp', axis=0, tiled=True)]
    dot_general x7 -> x0, matrix products: 18.5 us -> none  [the longest x1 5.74 us: on_device(): jnp.dot(lax.all_gather(normed, 'mp', axis=0, tiled=True), projector, pref...]
    all_to_all x1 -> x0, starting transfers between devices: 13.1 us -> none  [on_device(): lax.all_to_all(outgoing, 'dp', split_axis=0, concat_axis=0, tiled=True)]
    convert_element_type x7 -> x0, local copies, waits for them, and re-layouts: 10.1 us -> none  [the longest x4 5.32 us: subsample(): hidden = jnp.maximum(hidden, 0.0).astype(jnp.bfloat16)]
    conv_general_dilated x2 -> x0, matrix products: 9.92 us -> none  [the longest x1 5.12 us: subsample(): lax.conv_general_dilated(log_image[:, None], conv_first, (2, 2), ((1, 1),...]
  transfers between devices with their start and end apart: 3 -> 2, of which waited for: 3 -> 1; matrix products, arithmetic and copies ran while one was open for 4% -> 1% of each run, Pallas kernels for 0% -> 45%
where the time goes in v2:
time: 117 us; the launch traced here: 116 us
  Pallas kernels  54.1 us (46%)
  waiting for transfers between devices  39.9 us (34%)
  between operations  13.5 us (12%)
  local copies, waits for them, and re-layouts  7.39 us (6%)
    all_gather x1, waiting for transfers between devices, on_device(): near = lax.all_gather(own_half, 'mp', axis=0, tiled=True)  39.9 us
    pallas_call x1, Pallas kernels, on_device(): pl.pallas_call(functools.partial(block_kernel, mp_count), out_shape=(shap...  28.8 us
    pallas_call x1, Pallas kernels, on_device(): pl.pallas_call(functools.partial(frontend_kernel, dp_count), out_shape=(s...  23.6 us
    unnamed x20, local copies, waits for them, and re-layouts  5.83 us
  transfers between devices with their start and end apart: 2, of which 1 were waited for; matrix products, arithmetic and copies ran while one was open for 1% of the time, Pallas kernels for 45%

profile of v2, /device:TPU:1, one launch (start us, length us, event | category | flops | bytes accessed | tf_op | source)
XLA Modules:
  0.0 115.5 jit_solution(16097017895422307629)
XLA Ops:
  6.5 0.0 copy-start
  6.5 0.0 copy-start.2
  6.5 0.0 all-gather.2.cloned.1.call-start
  6.5 1.3 %copy-done = bf16[384,1536]{1,0:T(8,128)(2,1)S(1)} copy-done((bf16[384,1536]{1,0:T(8,128)(2,1)S(1)}, bf16[384,1536]{1,0:T(8,128)(2,1)}, u32[]{:S(2)}) %copy-start) | copy-done | bytes 1179672
  7.8 0.9 constant_dynamic-slice_fusion
  8.7 0.0 all-gather.2.cloned.1.call-update
  8.7 39.9 %all-gather.2.cloned.1.call-done.near = bf16[1536,768]{1,0:T(8,128)(2,1)} async-done(((bf16[384,768]{1,0:T(8,128)(2,1)}), bf16[1536,768]{1,0:T(8,128)(2,1)}) %all-gather.2.cloned.1.call-update) | async-done | bytes 2359312 | tf_op jit(solution)/shard_map/all_gather | solution.py:442
  48.6 0.7 collective-permute-start
  49.3 0.7 reshape.6.norm_gain
  50.0 0.0 copy-done.2
  50.0 0.0 copy-start.3
  50.0 1.0 copy-done.3
  51.0 0.0 copy-start.4
  51.0 0.9 copy-done.4
  51.9 0.0 copy-start.5
  51.9 0.7 copy-done.5
  52.5 0.0 copy-start.6
  52.5 0.7 copy-done.6
  53.2 0.0 copy-start.8
  53.2 0.7 copy-done.8
  53.9 0.0 copy-start.9
  53.9 0.7 copy-done.9
  54.5 0.0 copy-start.7
  54.5 23.6 %frontend.1 = (bf16[128,640]{1,0:T(8,128)(2,1)S(1)}, bf16[256,2560]{1,0:T(8,128)(2,1)S(1)}, bf16[3,640,256]{2,1,0:T(8,128)(2,1)S(1)}, bf16[1280,1536]{1,0:T(8,128)(2,1)}, bf16[3,1536,384]{2,1,0:T(8,128)(2,1)}) custom-call(bf16[4,41216]{1,0:T(4,128)(2,1)S(1)} %bitcast.13, s32[4]{0:T(128)S(1)} %bitcast.18, s32[4,64]{1,0:T(4,128)S(1)} %bitcast.16, ...), custom_call_target="tpu_custom_call" | custom-call | tf_op jit(solution)/shard_map/frontend/pallas_call | solution.py:445
  78.1 0.0 copy-done.7
  78.1 0.0 copy-start.1
  78.2 28.8 %block.1 = (bf16[4,128,384]{2,1,0:T(8,128)(2,1)S(1)}, bf16[128,1536]{1,0:T(8,128)(2,1)S(1)}) custom-call(bf16[128,640]{1,0:T(8,128)(2,1)S(1)} %get-tuple-element.12.own_windows, bf16[256,2560]{1,0:T(8,128)(2,1)S(1)} %get-tuple-element.13.first_table, bf16[3,640,256]{2,1,0:T(8,128)(2,1)S(1)} %get-tuple-element.14.second_table, ...), custom_call_target="tpu_custom_call" | custom-call | tf_op jit(solution)/shard_map/block/pallas_call | solution.py:483
  106.9 0.0 collective-permute-done.far
  106.9 0.0 copy-done.1
  106.9 1.7 %output.1 = bf16[128,1536]{1,0:T(8,128)(2,1)} custom-call(bf16[4,128,384]{2,1,0:T(8,128)(2,1)S(1)} %get-tuple-element.17.contexts, bf16[1536,768]{1,0:T(8,128)(2,1)S(1)} %copy-done.1, bf16[1536,768]{1,0:T(8,128)(2,1)S(1)} %collective-permute-done.far, bf16[128,1536]{1,0:T(8,128)(2,1)S(1)} %get-tuple-element.18.residual), custom_call_target="tpu_custom_call" | custom-call | tf_op jit(solution)/shard_map/output/pallas_call | solution.py:514
Async XLA Ops:
  6.5 1.3 %copy-start = (bf16[384,1536]{1,0:T(8,128)(2,1)S(1)}, bf16[384,1536]{1,0:T(8,128)(2,1)}, u32[]{:S(2)}) copy-start(bf16[384,1536]{1,0:T(8,128)(2,1)} %param.20) | copy-start | bytes 3538948
  6.5 43.4 %copy-start.2 = (bf16[4,256,640]{2,1,0:T(8,128)(2,1)S(1)}, bf16[4,256,640]{2,1,0:T(8,128)(2,1)}, u32[]{:S(2)}) copy-start(bf16[4,256,640]{2,1,0:T(8,128)(2,1)} %constant.21.clone.mel_hbm) | copy-start | bytes 3932164
  6.5 42.1 %all-gather.2.cloned.1.call-start = ((), (), s32[]{:S(2)}) async-start(), calls=%async_computation | async-start | bytes 2949120 | tf_op jit(solution)/shard_map/all_gather | solution.py:442
  48.6 58.3 %collective-permute-start = (bf16[1536,768]{1,0:T(8,128)(2,1)}, bf16[1536,768]{1,0:T(8,128)(2,1)S(1)}, u32[]{:S(2)}, u32[]{:S(2)}) collective-permute-start(bf16[1536,768]{1,0:T(8,128)(2,1)} %all-gather.2.cloned.1.call-done.near), channel_id=1, source_target_pairs={{0,4},{4,0},{8,12},{12,8},{16,20},{20,16},{24,28},{28,24},{32,36},... | collective-permute-start | bytes 7077896 | tf_op jit(solution)/shard_map/ppermute | solution.py:443
  50.0 1.0 copy-start.3
  51.0 0.9 copy-start.4
  51.9 0.7 copy-start.5
  52.5 0.7 copy-start.6
  53.2 0.7 copy-start.8
  53.9 0.7 copy-start.9
  54.5 23.6 %copy-start.7 = (s32[1,4,128]{2,1,0:T(4,128)S(1)}, s32[1,4,128]{2,1,0:T(4,128)}, u32[]{:S(2)}) copy-start(s32[1,4,128]{2,1,0:T(4,128)} %param.23) | copy-start | bytes 6148
  78.1 28.8 %copy-start.1 = (bf16[1536,768]{1,0:T(8,128)(2,1)S(1)}, bf16[1536,768]{1,0:T(8,128)(2,1)}, u32[]{:S(2)}) copy-start(bf16[1536,768]{1,0:T(8,128)(2,1)} %all-gather.2.cloned.1.call-done.near) | copy-start | bytes 7077892
Sparse Core Ops, SparseCore 0:
  9.2 39.3 all-gather.1

commit v3 on v2

v3 whole, which is shorter than its diff:
```python
import functools
import math

import jax
import jax.numpy as jnp
import ml_dtypes
import numpy as np
from jax import lax
from jax.experimental import pallas as pl
from jax.experimental.pallas import tpu as pltpu
from jax.sharding import PartitionSpec as P

N_MEL = 80
N_FFT = 400
HOP = 160
HEAD_DIM = 64
SLOT_ROWS = 64
CH = 64
MEL_HALF = 40
MEL_SUB = 20
STEP = 4 * HOP
ROW = 4 * N_MEL
WINDOW = 2 * ROW
MESH = pl.DeviceIdType.MESH
VMEM = pltpu.VMEM
BF16 = jnp.bfloat16
F32 = jnp.float32


def dft_table():
    position = np.arange(N_FFT)[:, None]
    harmonic = np.arange(256)[None, :]
    angles = 2.0 * math.pi * ((position * harmonic) % N_FFT) / N_FFT
    window = (0.5 - 0.5 * np.cos(2.0 * math.pi * position / N_FFT)) / math.sqrt(N_FFT)
    inside = harmonic <= N_FFT // 2
    base = np.concatenate(
        [np.where(inside, np.cos(angles), 0.0), np.where(inside, -np.sin(angles), 0.0)], axis=1
    )
    table = np.zeros((4, 512, 512))
    for r in range(4):
        table[r, 32 * r : 32 * r + N_FFT] = base * window
    return table.astype(ml_dtypes.bfloat16)


def mel_table():
    frequency = np.arange(N_FFT // 2 + 1) * (16000.0 / N_FFT)
    mel_top = 2595.0 * math.log10(1.0 + 8000.0 / 700.0)
    points = np.arange(N_MEL + 2) * (mel_top / (N_MEL + 1))
    hertz = 700.0 * (10.0 ** (points / 2595.0) - 1.0)
    lower, centre, upper = hertz[:-2], hertz[1:-1], hertz[2:]
    rising = (frequency[:, None] - lower) / (centre - lower)
    falling = (upper - frequency[:, None]) / (upper - centre)
    weights = np.maximum(0.0, np.minimum(rising, falling))
    table = np.zeros((4, 256, WINDOW))
    for r in range(4):
        for half in range(2):
            start = half * ROW + r * N_MEL
            table[r, : N_FFT // 2 + 1, start : start + N_MEL] = weights
    return table.astype(ml_dtypes.bfloat16)


def dot(a, b):
    return jnp.dot(a, b, preferred_element_type=F32)


def one_hot(condition):
    return condition.astype(F32).astype(BF16)


def iota(shape, dimension):
    return lax.broadcasted_iota(jnp.int32, shape, dimension)


def contract(a, b, dim_a, dim_b):
    return lax.dot_general(a, b, (((dim_a,), (dim_b,)), ((), ())), preferred_element_type=F32)


def solution_kernel(
    dp_count,
    mp_count,
    wave_hbm,
    lengths_hbm,
    picks_hbm,
    arrivals_hbm,
    first_hbm,
    second_hbm,
    dft_hbm,
    mel_hbm,
    weight_hbm,
    gain_hbm,
    attention_hbm,
    output_hbm,
    ids_hbm,
    encoded,
    wave,
    lengths,
    picks,
    arrivals,
    conv_first,
    conv_second,
    dft,
    mel,
    raw,
    norm_gain,
    attention,
    near,
    far,
    ids,
    first_table,
    second_table,
    weight,
    samples,
    slots_rows,
    outgoing,
    incoming,
    windows,
    shifted,
    hidden,
    features,
    embedded,
    normed,
    projected,
    sending,
    contexts,
    load_sems,
    exchange_send,
    exchange_recv,
    gather_send,
    gather_recv,
    near_send,
    near_recv,
    far_send,
    far_recv,
    context_send,
    context_recv,
):
    dp, me = lax.axis_index("dp"), lax.axis_index("mp")
    core = lax.rem(dp, 2)
    capacity = picks.shape[0]
    utterances = wave.shape[0]
    frames = utterances * SLOT_ROWS
    slots = dp_count * capacity
    per_block = windows.shape[1]
    rows = mp_count * per_block
    model = weight.shape[1]
    local = attention.shape[2]
    half = model // 2
    width = MEL_HALF * CH

    barrier = pltpu.get_barrier_semaphore()

    @pl.loop(1, dp_count)
    def _(d):
        pl.semaphore_signal(
            barrier, inc=1, device_id=(lax.rem(dp + d, dp_count), me), device_id_type=MESH
        )

    for d in range(1, mp_count):
        pl.semaphore_signal(
            barrier, inc=1, device_id=(dp, lax.rem(me + d, mp_count)), device_id_type=MESH
        )

    own_output = output_hbm.at[:, pl.ds(pl.multiple_of(core * half, 128), half)]
    loads = [
        pltpu.make_async_copy(source, target, load_sems.at[index])
        for index, (source, target) in enumerate(
            (
                (wave_hbm, wave),
                (dft_hbm, dft),
                (mel_hbm, mel),
                (lengths_hbm, lengths),
                (picks_hbm, picks),
                (first_hbm, conv_first),
                (second_hbm, conv_second),
                (arrivals_hbm, arrivals),
                (ids_hbm, ids),
                (gain_hbm, norm_gain),
                (weight_hbm, raw),
                (attention_hbm, attention),
                (own_output, near.at[0]),
            )
        )
    ]
    for load in loads:
        load.start()

    loads[0].wait()
    for s in range(SLOT_ROWS):
        samples[utterances * s : utterances * (s + 1), :] = wave[:, STEP * s : STEP * s + 896]
    loads[1].wait()
    loads[2].wait()
    energy = jnp.zeros((frames, WINDOW), F32)
    for r in range(4):
        spectrum = dot(samples[:, 128 * r : 128 * r + 512], dft[r])
        power = spectrum[:, :256] * spectrum[:, :256] + spectrum[:, 256:] * spectrum[:, 256:]
        energy += dot(power.astype(BF16), mel[r])
    loads[3].wait()
    row = iota((frames, 1), 0)
    limit = jnp.broadcast_to(lengths[0:1, 0:1], (frames, 1))
    for u in range(1, utterances):
        limit = jnp.where(row % utterances == u, lengths[0:1, u : u + 1], limit)
    image = jnp.where(row // utterances < limit, jnp.log(energy + 0.01), 0.0).astype(BF16)

    loads[4].wait()
    target = (dp + iota((slots, dp_count), 0) // capacity) % dp_count
    chosen = contract(
        one_hot(iota((slots, dp_count), 1) == target), picks[...].astype(F32).astype(BF16), 1, 1
    )
    chosen = jnp.where(
        iota((slots, capacity), 1) == iota((slots, capacity), 0) % capacity, chosen, 0.0
    )
    pick = jnp.sum(chosen, axis=1, keepdims=True).astype(jnp.int32)
    place = jnp.where(pick < 0, -SLOT_ROWS, pick % SLOT_ROWS * utterances + pick // SLOT_ROWS)
    column = iota((slots, frames), 1)
    own = dot(one_hot(column == place), image)
    earlier = dot(one_hot(column == place - utterances), image)
    slots_rows[...] = jnp.where(iota(own.shape, 1) < ROW, earlier, own)
    for d in range(dp_count):
        slab = slots_rows[capacity * d : capacity * (d + 1), :].astype(BF16)
        if d == 0:
            incoming[0] = slab
        else:
            outgoing[d] = slab

    pl.semaphore_wait(barrier, dp_count - 1 + mp_count - 1)

    def exchange(d):
        return pltpu.make_async_remote_copy(
            src_ref=outgoing.at[d],
            dst_ref=incoming.at[d],
            send_sem=exchange_send.at[d],
            recv_sem=exchange_recv.at[d],
            device_id=(lax.rem(dp + d, dp_count), me),
            device_id_type=MESH,
        )

    def to_lane(source, target, send_sem, recv_sem, d):
        return pltpu.make_async_remote_copy(
            src_ref=source,
            dst_ref=target,
            send_sem=send_sem,
            recv_sem=recv_sem,
            device_id=(dp, lax.rem(me + d, mp_count)),
            device_id_type=MESH,
        )

    def to_sibling(d):
        return pltpu.make_async_remote_copy(
            src_ref=near.at[d],
            dst_ref=far.at[d],
            send_sem=far_send.at[d],
            recv_sem=far_recv.at[d],
            device_id=(dp + 1 - 2 * core, me),
            device_id_type=MESH,
        )

    @pl.loop(1, dp_count)
    def _(d):
        exchange(d).start()

    last = mp_count - 1
    share = local // 2
    near_out = [
        to_lane(own_output, near.at[last], near_send.at[0], near_recv.at[0], 1),
        to_lane(own_output, near.at[1], near_send.at[1], near_recv.at[1], last),
    ]
    near_on = [
        to_lane(near.at[last, :share], near.at[2, :share], near_send.at[2], near_recv.at[2], 1),
        to_lane(near.at[1, share:], near.at[2, share:], near_send.at[3], near_recv.at[3], last),
    ]
    for copy in near_out:
        copy.start()

    loads[5].wait()
    loads[6].wait()
    twice = one_hot(iota((CH, 2 * CH), 0) == iota((CH, 2 * CH), 1) % CH)
    taps = [dot(conv_first[d], twice) for d in range(3)]
    first_table[3 * N_MEL :, :] = jnp.zeros((256 - 3 * N_MEL, width), BF16)
    offset = iota((N_MEL, 2 * CH), 0) - 2 * (iota((N_MEL, 2 * CH), 1) // CH) + 1
    for n in range(MEL_HALF // 2):
        for t in range(3):
            block = jnp.zeros(offset.shape, F32)
            for d in range(3):
                block = jnp.where(offset - 4 * n == d, taps[d][t : t + 1, :], block)
            first_table[t * N_MEL : (t + 1) * N_MEL, 2 * CH * n : 2 * CH * (n + 1)] = block.astype(BF16)
    spread = one_hot(iota((CH, 4 * CH), 0) == iota((CH, 4 * CH), 1) // 4)
    sub_band = iota((CH, 4 * CH), 1) % 4
    for t in range(3):
        wide = [contract(conv_second[d, t], spread, 0, 0) for d in range(3)]
        for k in range(10):
            block = jnp.zeros((CH, 4 * CH), F32)
            for d in range(3):
                block = jnp.where(2 * sub_band + d + 1 == k, wide[d], block)
            second_table[t, k * CH : (k + 1) * CH, :] = block.astype(BF16)
    span = 16 * MEL_SUB
    out_row, in_row = iota((span, span), 0), iota((span, span), 1)
    source = (out_row % 64 // 4) * MEL_SUB + out_row // 64 * 4 + out_row % 4
    order = one_hot(in_row == source)
    loads[10].wait()
    for block in range(4):
        value = dot(order, raw[block * span : (block + 1) * span, :]).astype(BF16)
        for g in range(5):
            weight[256 * g + 64 * block : 256 * g + 64 * (block + 1), :] = value[64 * g : 64 * (g + 1), :]
    shifted[:, :, 3 * N_MEL :] = jnp.zeros((3, rows, 256 - 3 * N_MEL), BF16)
    hidden[:, :, :128] = jnp.zeros((3, rows, 128), BF16)

    loads[7].wait()
    loads[8].wait()
    loads[9].wait()
    loads[11].wait()
    loads[12].wait()
    arrival = arrivals[...]
    position = (dp + dp_count - arrival // capacity) % dp_count * capacity + arrival % capacity
    take = (iota((slots, per_block), 0) == position).astype(F32)
    take = jnp.transpose(take).astype(BF16)

    @pl.loop(1, dp_count)
    def _(d):
        exchange(d).wait_recv()

    for d in range(dp_count):
        slots_rows[capacity * d : capacity * (d + 1), :] = incoming[d].astype(F32)
    windows[0] = dot(take, slots_rows[...].astype(BF16)).astype(BF16)

    middle = per_block // 2
    window_out = [
        to_lane(windows.at[0], windows.at[last], gather_send.at[0], gather_recv.at[0], 1),
        to_lane(windows.at[0], windows.at[1], gather_send.at[1], gather_recv.at[1], last),
    ]
    window_on = [
        to_lane(windows.at[last, :middle], windows.at[2, :middle], gather_send.at[2], gather_recv.at[2], 1),
        to_lane(windows.at[1, middle:], windows.at[2, middle:], gather_send.at[3], gather_recv.at[3], last),
    ]
    for copy in window_out:
        copy.start()

    def convolve(start, stop, image):
        span = slice(start, stop)
        for t in range(3):
            first = (1 + 2 * t) * N_MEL
            shifted[t, span, : 3 * N_MEL] = image[:, first : first + 3 * N_MEL]
        for t in range(3):
            for n in range(width // 256):
                value = dot(shifted[t, span, :], first_table[:, n * 256 : (n + 1) * 256])
                hidden[t, span, 128 + n * 256 : 128 + (n + 1) * 256] = jnp.maximum(value, 0.0).astype(BF16)
        for g in range(5):
            value = dot(hidden[0, span, 512 * g : 512 * g + 640], second_table[0])
            value += dot(hidden[1, span, 512 * g : 512 * g + 640], second_table[1])
            value += dot(hidden[2, span, 512 * g : 512 * g + 640], second_table[2])
            features[span, 256 * g : 256 * (g + 1)] = jnp.maximum(value, 0.0).astype(BF16)

    def project(start, stop):
        span = slice(start, stop)
        for n in range(model // 256):
            embedded[span, n * 256 : (n + 1) * 256] = dot(
                features[span, :], weight[:, n * 256 : (n + 1) * 256]
            ).astype(BF16)
        gain = norm_gain[...].reshape(1, model)
        for b in range(start, stop, per_block):
            values = embedded[b : b + per_block, :].astype(F32)
            centre = values - jnp.mean(values, axis=-1, keepdims=True)
            variance = jnp.mean(centre * centre, axis=-1, keepdims=True)
            normed[b : b + per_block, :] = (centre * lax.rsqrt(variance + 1e-05) * gain).astype(BF16)
        for part in range(3):
            projected[part, span, :] = dot(normed[span, :], attention[part]).astype(BF16)

    lower = iota((per_block, 128), 1) < HEAD_DIM
    zero = jnp.zeros((per_block, 128), BF16)

    def attend(b, target):
        block_ids = ids[pl.ds(lax.rem(me + b, mp_count), 1), :]
        across = jnp.broadcast_to(block_ids, (per_block, per_block))
        same = across == jnp.transpose(across)
        span = slice(b * per_block, (b + 1) * per_block)
        for pair in range(local // 128):
            lanes = slice(pair * 128, (pair + 1) * 128)
            query = projected[0, span, lanes]
            key = projected[1, span, lanes]
            value = projected[2, span, lanes]
            key_pair = jnp.concatenate(
                [jnp.where(lower, key, zero), jnp.where(lower, zero, key)], axis=0
            )
            value_pair = jnp.concatenate(
                [jnp.where(lower, value, zero), jnp.where(lower, zero, value)], axis=0
            )
            scores = contract(query, key_pair, 1, 1) * (1.0 / math.sqrt(HEAD_DIM))
            weights = []
            for side in range(2):
                part = jnp.where(same, scores[:, side * per_block : (side + 1) * per_block], -jnp.inf)
                largest = jnp.max(part, axis=-1, keepdims=True)
                exponent = jnp.exp(part - largest)
                total = jnp.sum(exponent, axis=-1, keepdims=True)
                weights.append((exponent / total).astype(BF16))
            target[b, :, lanes] = dot(jnp.concatenate(weights, axis=1), value_pair).astype(BF16)

    convolve(0, per_block, windows[0])
    for copy in window_out:
        copy.wait_recv()
    for copy in window_on:
        copy.start()
    project(0, per_block)
    attend(0, contexts)
    for copy in window_on:
        copy.wait_recv()
    for copy in near_out:
        copy.wait_recv()
    for copy in near_on:
        copy.start()
    for d in (0, 1, last):
        to_sibling(d).start()
    convolve(per_block, rows, windows[1:].reshape(rows - per_block, WINDOW))
    project(per_block, rows)
    context_out = {}
    for d in (2, 1, last):
        attend(d, sending)
        context_out[d] = to_lane(
            sending.at[d],
            contexts.at[mp_count - d],
            context_send.at[d],
            context_recv.at[mp_count - d],
            d,
        )
        context_out[d].start()
    for copy in near_on:
        copy.wait_recv()
    to_sibling(2).start()
    for d in range(mp_count):
        to_sibling(d).wait_recv()

    sides = [embedded[:per_block, pl.ds(pl.multiple_of(index * half, 128), half)].astype(F32) for index in (core, 1 - core)]
    for d in (0, 2, 1, last):
        if d:
            to_lane(sending.at[d], contexts.at[d], context_send.at[d], context_recv.at[d], d).wait_recv()
        for index, part in enumerate((near, far)):
            sides[index] += dot(contexts[d], part[d])
    for index, value in zip((core, 1 - core), sides):
        encoded[:, pl.ds(pl.multiple_of(index * half, 128), half)] = value.astype(BF16)

    @pl.loop(1, dp_count)
    def _(d):
        exchange(d).wait_send()

    for copy in window_out + window_on + near_out + near_on + list(context_out.values()):
        copy.wait_send()
    for d in range(mp_count):
        to_sibling(d).wait_send()


def on_device(
    dp_count,
    mp_count,
    waveform,
    lengths,
    conv_first,
    conv_second,
    input_weight,
    norm_gain,
    attention_in,
    attention_out,
    send_slots,
    receive_slots,
    segment_ids,
):
    capacity = send_slots.shape[3]
    utterances = waveform.shape[2]
    per_block = receive_slots.shape[2]
    model = input_weight.shape[1]
    local = attention_in.shape[2]
    half = model // 2
    rows = mp_count * per_block
    slots = dp_count * capacity
    dma = pltpu.SemaphoreType.DMA
    operands = (
        waveform[0, 0],
        lengths[0],
        send_slots[0, :, 0, :].transpose(1, 0),
        receive_slots[0],
        conv_first.transpose(1, 2, 3, 0)[0],
        conv_second.transpose(2, 3, 0, 1),
        jnp.asarray(dft_table()),
        jnp.asarray(mel_table()),
        input_weight,
        norm_gain,
        attention_in.transpose(1, 0, 2),
        attention_out,
        segment_ids[0],
    )
    encoded = pl.pallas_call(
        functools.partial(solution_kernel, dp_count, mp_count),
        out_shape=jax.ShapeDtypeStruct((per_block, model), BF16),
        in_specs=[pl.BlockSpec(memory_space=pltpu.HBM)] * len(operands),
        out_specs=pl.BlockSpec(memory_space=VMEM),
        scratch_shapes=[
            VMEM(waveform.shape[2:], BF16),
            VMEM((1, utterances), jnp.int32),
            VMEM((capacity, dp_count), jnp.int32),
            VMEM((1, per_block), jnp.int32),
            VMEM((3, 3, CH), BF16),
            VMEM((3, 3, CH, CH), BF16),
            VMEM((4, 512, 512), BF16),
            VMEM((4, 256, WINDOW), BF16),
            VMEM((CH * MEL_SUB, model), BF16),
            VMEM((model,), F32),
            VMEM((3, model, local), BF16),
            VMEM((mp_count, local, half), BF16),
            VMEM((mp_count, local, half), BF16),
            VMEM((mp_count, per_block), jnp.int32),
            VMEM((256, MEL_HALF * CH), BF16),
            VMEM((3, 10 * CH, 4 * CH), BF16),
            VMEM((CH * MEL_SUB, model), BF16),
            VMEM((utterances * SLOT_ROWS, 896), BF16),
            VMEM((slots, WINDOW), F32),
            VMEM((dp_count, capacity, WINDOW), BF16),
            VMEM((dp_count, capacity, WINDOW), BF16),
            VMEM((mp_count, per_block, WINDOW), BF16),
            VMEM((3, rows, 256), BF16),
            VMEM((3, rows, 128 + MEL_HALF * CH), BF16),
            VMEM((rows, CH * MEL_SUB), BF16),
            VMEM((rows, model), BF16),
            VMEM((rows, model), BF16),
            VMEM((3, rows, local), BF16),
            VMEM((mp_count, per_block, local), BF16),
            VMEM((mp_count, per_block, local), BF16),
            dma((13,)),
            dma((dp_count,)),
            dma((dp_count,)),
            dma((4,)),
            dma((4,)),
            dma((4,)),
            dma((4,)),
            dma((mp_count,)),
            dma((mp_count,)),
            dma((mp_count,)),
            dma((mp_count,)),
        ],
        compiler_params=pltpu.CompilerParams(
            vmem_limit_bytes=60 * 2**20, collective_id=0, has_side_effects=True
        ),
        name="encode",
    )(*operands)
    return encoded.reshape(1, 1, per_block, model)


def solution(mesh):
    return jax.shard_map(
        functools.partial(on_device, mesh.shape["dp"], mesh.shape["mp"]),
        mesh=mesh,
        in_specs=(
            P("dp", "mp", None, None),
            P("dp", "mp", None),
            P(),
            P(),
            P(),
            P(),
            P(None, None, "mp"),
            P("mp", None),
            P("dp", None, "mp", None),
            P("dp", "mp", None),
            P("dp", None, None),
        ),
        out_specs=P("dp", "mp", None, None),
        check_vma=False,
    )
```

time: 117 us -> 54.4 us (0.46); the launches traced: 116 us -> 54.3 us
  waiting for transfers between devices: 39.9 us -> 0 us
  between operations: 13.5 us -> 0.01 us
  local copies, waits for them, and re-layouts: 7.39 us -> 1.77 us
  Pallas kernels: 54.1 us -> 52.5 us
    all_gather x1 -> x0, waiting for transfers between devices: 39.9 us -> none  [on_device(): near = lax.all_gather(own_half, 'mp', axis=0, tiled=True)]
    unnamed x20 -> x1, local copies, waits for them, and re-layouts: 5.83 us -> 1.77 us
    pallas_call x3 -> x1, Pallas kernels: 54.1 us -> 52.5 us  [on_device(): pl.pallas_call(functools.partial(solution_kernel, dp_count, mp_count), ou...]
  transfers between devices with their start and end apart: 2 -> 0, of which waited for: 1 -> 0; matrix products, arithmetic and copies ran while one was open for 1% -> 0% of each run, Pallas kernels for 45% -> 0%
where the time goes in v3:
time: 54.4 us; the launch traced here: 54.3 us
  Pallas kernels  52.5 us (97%)
  local copies, waits for them, and re-layouts  1.77 us (3%)
    pallas_call x1, Pallas kernels, on_device(): pl.pallas_call(functools.partial(solution_kernel, dp_count, mp_count), ou...  52.5 us
    unnamed x1, local copies, waits for them, and re-layouts  1.77 us

profile of v3, /device:TPU:1, one launch (start us, length us, event | category | flops | bytes accessed | tf_op | source)
XLA Modules:
  0.0 54.3 jit_solution(13581376369630698290)
XLA Ops:
  0.0 52.5 %encode.1 = bf16[128,1536]{1,0:T(8,128)(2,1)} custom-call(bf16[4,41216]{1,0:T(4,128)(2,1)} %bitcast.15, s32[1,4]{1,0:T(1,128)} %bitcast.20, s32[4,64]{1,0:T(4,128)} %bitcast.18, s32[1,128]{1,0:T(1,128)} %bitcast.21, bf16[3,3,64]{2,1,0:T(4,128)(2,1)} %bitcast.17, bf16[3,3,64,64]{3,2,1,0:T(8,128)(2,1)} %bitcast.16, ...), custom_call_target="tpu_custom_call" | custom-call | tf_op jit(solution)/shard_map/encode/pallas_call | solution.py:488
  52.5 1.8 %copy.15 = bf16[1,1,128,1536]{3,2,1,0:T(8,128)(2,1)} copy(bf16[1,1,128,1536]{3,2,1,0:T(8,128)(2,1)} %bitcast.14) | data formatting | bytes 786432

commit v4 on v3

--- a/solution.py
+++ b/solution.py
@@ -21,6 +21,7 @@
 STEP = 4 * HOP
 ROW = 4 * N_MEL
 WINDOW = 2 * ROW
+X_CHIPS = 4
 MESH = pl.DeviceIdType.MESH
 VMEM = pltpu.VMEM
 BF16 = jnp.bfloat16
@@ -129,6 +130,8 @@
     gather_recv,
     near_send,
     near_recv,
+    ring_send,
+    ring_recv,
     far_send,
     far_recv,
     context_send,
@@ -143,9 +146,33 @@
     per_block = windows.shape[1]
     rows = mp_count * per_block
     model = weight.shape[1]
-    local = attention.shape[2]
+    local = attention.shape[1] // 3
     half = model // 2
     width = MEL_HALF * CH
+
+    own_output = output_hbm.at[:, pl.ds(pl.multiple_of(core * half, 128), half)]
+    plan = [
+        (wave_hbm, wave),
+        (dft_hbm, dft),
+        (mel_hbm, mel),
+        (lengths_hbm, lengths),
+        (picks_hbm, picks),
+        (first_hbm, conv_first),
+        (second_hbm, conv_second),
+        (arrivals_hbm, arrivals),
+        (ids_hbm, ids),
+        (gain_hbm, norm_gain),
+        (weight_hbm, raw),
+        (own_output, near.at[0]),
+    ]
+    for part in range(3):
+        plan.append((attention_hbm.at[part], attention.at[:, part * local : (part + 1) * local]))
+    loads = [
+        pltpu.make_async_copy(source, target, load_sems.at[index])
+        for index, (source, target) in enumerate(plan)
+    ]
+    for load in loads[:5]:
+        load.start()
 
     barrier = pltpu.get_barrier_semaphore()
 
@@ -160,28 +187,7 @@
             barrier, inc=1, device_id=(dp, lax.rem(me + d, mp_count)), device_id_type=MESH
         )
 
-    own_output = output_hbm.at[:, pl.ds(pl.multiple_of(core * half, 128), half)]
-    loads = [
-        pltpu.make_async_copy(source, target, load_sems.at[index])
-        for index, (source, target) in enumerate(
-            (
-                (wave_hbm, wave),
-                (dft_hbm, dft),
-                (mel_hbm, mel),
-                (lengths_hbm, lengths),
-                (picks_hbm, picks),
-                (first_hbm, conv_first),
-                (second_hbm, conv_second),
-                (arrivals_hbm, arrivals),
-                (ids_hbm, ids),
-                (gain_hbm, norm_gain),
-                (weight_hbm, raw),
-                (attention_hbm, attention),
-                (own_output, near.at[0]),
-            )
-        )
-    ]
-    for load in loads:
+    for load in loads[5:]:
         load.start()
 
     loads[0].wait()
@@ -244,32 +250,74 @@
             device_id_type=MESH,
         )
 
-    def to_sibling(d):
+    stride = dp_count // X_CHIPS
+    ring = dp // stride
+    quarter = local // 4
+    parity = lax.rem(ring, 2)
+
+    def quarter_rows(side, c, start=0, size=quarter):
+        first = (2 * side + c) * quarter + start
+        return pl.ds(pl.multiple_of(first, 16), size)
+
+    def part_copy(c, d):
+        rows = quarter_rows(parity, c)
+        return to_lane(
+            output_hbm.at[rows, pl.ds(pl.multiple_of(core * half, 128), half)],
+            near.at[mp_count - d, rows],
+            near_send.at[c, d],
+            near_recv.at[c, d],
+            d,
+        )
+
+    def ring_copy(c, step, side):
+        rows = quarter_rows(side, c, step * (quarter // 2), quarter // 2)
         return pltpu.make_async_remote_copy(
-            src_ref=near.at[d],
-            dst_ref=far.at[d],
-            send_sem=far_send.at[d],
-            recv_sem=far_recv.at[d],
+            src_ref=near.at[1:, rows],
+            dst_ref=near.at[1:, rows],
+            send_sem=ring_send.at[c, step],
+            recv_sem=ring_recv.at[c, step],
+            device_id=(lax.rem(dp + (1 - 2 * step) * stride + dp_count, dp_count), me),
+            device_id_type=MESH,
+        )
+
+    def to_sibling(index):
+        if index == 0:
+            source, target = near.at[0], far.at[0]
+        elif index < 3:
+            rows = quarter_rows(parity, index - 1)
+            source, target = near.at[1:, rows], far.at[1:, rows]
+        else:
+            c, step = (index - 3) // 2, (index - 3) % 2
+            rows = quarter_rows(1 - parity, c, step * (quarter // 2), quarter // 2)
+            source, target = near.at[1:, rows], far.at[1:, rows]
+        return pltpu.make_async_remote_copy(
+            src_ref=source,
+            dst_ref=target,
+            send_sem=far_send.at[index],
+            recv_sem=far_recv.at[index],
             device_id=(dp + 1 - 2 * core, me),
             device_id_type=MESH,
         )
+
+    def pass_on(c):
+        for d in range(1, mp_count):
+            part_copy(c, d).wait_recv()
+        for step in range(2):
+            ring_copy(c, step, parity).start()
+        to_sibling(1 + c).start()
+
+    def share_ring(c):
+        for step in range(2):
+            ring_copy(c, step, 1 - parity).wait_recv()
+            to_sibling(3 + 2 * c + step).start()
 
     @pl.loop(1, dp_count)
     def _(d):
         exchange(d).start()
 
-    last = mp_count - 1
-    share = local // 2
-    near_out = [
-        to_lane(own_output, near.at[last], near_send.at[0], near_recv.at[0], 1),
-        to_lane(own_output, near.at[1], near_send.at[1], near_recv.at[1], last),
-    ]
-    near_on = [
-        to_lane(near.at[last, :share], near.at[2, :share], near_send.at[2], near_recv.at[2], 1),
-        to_lane(near.at[1, share:], near.at[2, share:], near_send.at[3], near_recv.at[3], last),
-    ]
-    for copy in near_out:
-        copy.start()
+    for c in range(2):
+        for d in range(1, mp_count):
+            part_copy(c, d).start()
 
     loads[5].wait()
     loads[6].wait()
@@ -291,7 +339,8 @@
             block = jnp.zeros((CH, 4 * CH), F32)
             for d in range(3):
                 block = jnp.where(2 * sub_band + d + 1 == k, wide[d], block)
-            second_table[t, k * CH : (k + 1) * CH, :] = block.astype(BF16)
+            start = k // 2 * 384 + t * 128 + k % 2 * CH
+            second_table[start : start + CH, :] = block.astype(BF16)
     span = 16 * MEL_SUB
     out_row, in_row = iota((span, span), 0), iota((span, span), 1)
     source = (out_row % 64 // 4) * MEL_SUB + out_row // 64 * 4 + out_row % 4
@@ -302,17 +351,21 @@
         for g in range(5):
             weight[256 * g + 64 * block : 256 * g + 64 * (block + 1), :] = value[64 * g : 64 * (g + 1), :]
     shifted[:, :, 3 * N_MEL :] = jnp.zeros((3, rows, 256 - 3 * N_MEL), BF16)
-    hidden[:, :, :128] = jnp.zeros((3, rows, 128), BF16)
+    hidden[:, :384] = jnp.zeros((rows, 384), BF16)
 
     loads[7].wait()
     loads[8].wait()
     loads[9].wait()
     loads[11].wait()
     loads[12].wait()
+    loads[13].wait()
+    loads[14].wait()
     arrival = arrivals[...]
     position = (dp + dp_count - arrival // capacity) % dp_count * capacity + arrival % capacity
     take = (iota((slots, per_block), 0) == position).astype(F32)
     take = jnp.transpose(take).astype(BF16)
+    to_sibling(0).start()
+    pass_on(0)
 
     @pl.loop(1, dp_count)
     def _(d):
@@ -322,17 +375,18 @@
         slots_rows[capacity * d : capacity * (d + 1), :] = incoming[d].astype(F32)
     windows[0] = dot(take, slots_rows[...].astype(BF16)).astype(BF16)
 
-    middle = per_block // 2
-    window_out = [
-        to_lane(windows.at[0], windows.at[last], gather_send.at[0], gather_recv.at[0], 1),
-        to_lane(windows.at[0], windows.at[1], gather_send.at[1], gather_recv.at[1], last),
-    ]
-    window_on = [
-        to_lane(windows.at[last, :middle], windows.at[2, :middle], gather_send.at[2], gather_recv.at[2], 1),
-        to_lane(windows.at[1, middle:], windows.at[2, middle:], gather_send.at[3], gather_recv.at[3], last),
-    ]
-    for copy in window_out:
+    last = mp_count - 1
+    window_out = {
+        d: to_lane(
+            windows.at[0], windows.at[mp_count - d], gather_send.at[d], gather_recv.at[mp_count - d], d
+        )
+        for d in (1, last, 2)
+    }
+    for copy in window_out.values():
         copy.start()
+
+    def wait_window(d):
+        to_lane(windows.at[0], windows.at[d], gather_send.at[d], gather_recv.at[d], d).wait_recv()
 
     def convolve(start, stop, image):
         span = slice(start, stop)
@@ -342,11 +396,12 @@
         for t in range(3):
             for n in range(width // 256):
                 value = dot(shifted[t, span, :], first_table[:, n * 256 : (n + 1) * 256])
-                hidden[t, span, 128 + n * 256 : 128 + (n + 1) * 256] = jnp.maximum(value, 0.0).astype(BF16)
+                value = jnp.maximum(value, 0.0).astype(BF16)
+                for pair in range(2):
+                    lanes = 384 * (1 + 2 * n + pair) + 128 * t
+                    hidden[span, lanes : lanes + 128] = value[:, 128 * pair : 128 * (pair + 1)]
         for g in range(5):
-            value = dot(hidden[0, span, 512 * g : 512 * g + 640], second_table[0])
-            value += dot(hidden[1, span, 512 * g : 512 * g + 640], second_table[1])
-            value += dot(hidden[2, span, 512 * g : 512 * g + 640], second_table[2])
+            value = dot(hidden[span, 1536 * g : 1536 * g + 1920], second_table[...])
             features[span, 256 * g : 256 * (g + 1)] = jnp.maximum(value, 0.0).astype(BF16)
 
     def project(start, stop):
@@ -361,22 +416,24 @@
             centre = values - jnp.mean(values, axis=-1, keepdims=True)
             variance = jnp.mean(centre * centre, axis=-1, keepdims=True)
             normed[b : b + per_block, :] = (centre * lax.rsqrt(variance + 1e-05) * gain).astype(BF16)
-        for part in range(3):
-            projected[part, span, :] = dot(normed[span, :], attention[part]).astype(BF16)
+        for start in range(0, 3 * local, 256):
+            lanes = slice(start, min(start + 256, 3 * local))
+            projected[span, lanes] = dot(normed[span, :], attention[:, lanes]).astype(BF16)
 
     lower = iota((per_block, 128), 1) < HEAD_DIM
     zero = jnp.zeros((per_block, 128), BF16)
 
     def attend(b, target):
-        block_ids = ids[pl.ds(lax.rem(me + b, mp_count), 1), :]
+        d = (0, 1, last, 2)[b]
+        block_ids = ids[pl.ds(lax.rem(me + d, mp_count), 1), :]
         across = jnp.broadcast_to(block_ids, (per_block, per_block))
         same = across == jnp.transpose(across)
         span = slice(b * per_block, (b + 1) * per_block)
         for pair in range(local // 128):
             lanes = slice(pair * 128, (pair + 1) * 128)
-            query = projected[0, span, lanes]
-            key = projected[1, span, lanes]
-            value = projected[2, span, lanes]
+            query = projected[span, lanes]
+            key = projected[span, local + pair * 128 : local + (pair + 1) * 128]
+            value = projected[span, 2 * local + pair * 128 : 2 * local + (pair + 1) * 128]
             key_pair = jnp.concatenate(
                 [jnp.where(lower, key, zero), jnp.where(lower, zero, key)], axis=0
             )
@@ -393,42 +450,41 @@
                 weights.append((exponent / total).astype(BF16))
             target[b, :, lanes] = dot(jnp.concatenate(weights, axis=1), value_pair).astype(BF16)
 
-    convolve(0, per_block, windows[0])
-    for copy in window_out:
-        copy.wait_recv()
-    for copy in window_on:
-        copy.start()
-    project(0, per_block)
-    attend(0, contexts)
-    for copy in window_on:
-        copy.wait_recv()
-    for copy in near_out:
-        copy.wait_recv()
-    for copy in near_on:
-        copy.start()
-    for d in (0, 1, last):
-        to_sibling(d).start()
-    convolve(per_block, rows, windows[1:].reshape(rows - per_block, WINDOW))
-    project(per_block, rows)
     context_out = {}
-    for d in (2, 1, last):
-        attend(d, sending)
+
+    def share_contexts(d, block):
+        attend(block, sending)
         context_out[d] = to_lane(
-            sending.at[d],
+            sending.at[block],
             contexts.at[mp_count - d],
             context_send.at[d],
             context_recv.at[mp_count - d],
             d,
         )
         context_out[d].start()
-    for copy in near_on:
-        copy.wait_recv()
-    to_sibling(2).start()
-    for d in range(mp_count):
-        to_sibling(d).wait_recv()
+
+    convolve(0, per_block, windows[0])
+    pass_on(1)
+    project(0, per_block)
+    attend(0, contexts)
+    wait_window(1)
+    wait_window(last)
+    image = jnp.concatenate([windows[1], windows[last]], axis=0)
+    convolve(per_block, 3 * per_block, image)
+    wait_window(2)
+    project(per_block, 3 * per_block)
+    share_contexts(1, 1)
+    share_contexts(last, 2)
+    convolve(3 * per_block, rows, windows[2])
+    share_ring(0)
+    project(3 * per_block, rows)
+    share_ring(1)
+    share_contexts(2, 3)
+    for index in range(7):
+        to_sibling(index).wait_recv()
 
     sides = [embedded[:per_block, pl.ds(pl.multiple_of(index * half, 128), half)].astype(F32) for index in (core, 1 - core)]
-    for d in (0, 2, 1, last):
+    for d in (0, 1, last, 2):
         if d:
             to_lane(sending.at[d], contexts.at[d], context_send.at[d], context_recv.at[d], d).wait_recv()
         for index, part in enumerate((near, far)):
@@ -440,10 +496,15 @@
     def _(d):
         exchange(d).wait_send()
 
-    for copy in window_out + window_on + near_out + near_on + list(context_out.values()):
+    for copy in list(window_out.values()) + list(context_out.values()):
         copy.wait_send()
-    for d in range(mp_count):
-        to_sibling(d).wait_send()
+    for c in range(2):
+        for d in range(1, mp_count):
+            part_copy(c, d).wait_send()
+        for step in range(2):
+            ring_copy(c, step, parity).wait_send()
+    for index in range(7):
+        to_sibling(index).wait_send()
 
 
 def on_device(
@@ -501,12 +562,12 @@
             VMEM((4, 256, WINDOW), BF16),
             VMEM((CH * MEL_SUB, model), BF16),
             VMEM((model,), F32),
-            VMEM((3, model, local), BF16),
+            VMEM((model, 3 * local), BF16),
             VMEM((mp_count, local, half), BF16),
             VMEM((mp_count, local, half), BF16),
             VMEM((mp_count, per_block), jnp.int32),
             VMEM((256, MEL_HALF * CH), BF16),
-            VMEM((3, 10 * CH, 4 * CH), BF16),
+            VMEM((30 * CH, 4 * CH), BF16),
             VMEM((CH * MEL_SUB, model), BF16),
             VMEM((utterances * SLOT_ROWS, 896), BF16),
             VMEM((slots, WINDOW), F32),
@@ -514,22 +575,24 @@
             VMEM((dp_count, capacity, WINDOW), BF16),
             VMEM((mp_count, per_block, WINDOW), BF16),
             VMEM((3, rows, 256), BF16),
-            VMEM((3, rows, 128 + MEL_HALF * CH), BF16),
+            VMEM((rows, 384 + 3 * MEL_HALF * CH), BF16),
             VMEM((rows, CH * MEL_SUB), BF16),
             VMEM((rows, model), BF16),
             VMEM((rows, model), BF16),
-            VMEM((3, rows, local), BF16),
+            VMEM((rows, 3 * local), BF16),
             VMEM((mp_count, per_block, local), BF16),
             VMEM((mp_count, per_block, local), BF16),
-            dma((13,)),
+            dma((15,)),
             dma((dp_count,)),
             dma((dp_count,)),
-            dma((4,)),
-            dma((4,)),
-            dma((4,)),
-            dma((4,)),
             dma((mp_count,)),
             dma((mp_count,)),
+            dma((2, mp_count)),
+            dma((2, mp_count)),
+            dma((2, 2)),
+            dma((2, 2)),
+            dma((7,)),
+            dma((7,)),
             dma((mp_count,)),
             dma((mp_count,)),
         ],

time: 54.4 us -> 51.1 us (0.939)
  Pallas kernels: 52.5 us -> 49.2 us
    pallas_call x1, Pallas kernels: 52.5 us -> 49.2 us  [on_device(): pl.pallas_call(functools.partial(solution_kernel, dp_count, mp_count), ou...]
where the time goes in v4:
time: 51.1 us; the launch traced here: 51 us
  Pallas kernels  49.2 us (96%)
  local copies, waits for them, and re-layouts  1.77 us (3%)
    pallas_call x1, Pallas kernels, on_device(): pl.pallas_call(functools.partial(solution_kernel, dp_count, mp_count), ou...  49.2 us
    unnamed x1, local copies, waits for them, and re-layouts  1.77 us

profile of v4, /device:TPU:1, one launch (start us, length us, event | category | flops | bytes accessed | tf_op | source)
XLA Modules:
  0.0 51.0 jit_solution(11459871640367577636)
XLA Ops:
  0.0 49.2 %encode.1 = bf16[128,1536]{1,0:T(8,128)(2,1)} custom-call(bf16[4,41216]{1,0:T(4,128)(2,1)} %bitcast.15, s32[1,4]{1,0:T(1,128)} %bitcast.20, s32[4,64]{1,0:T(4,128)} %bitcast.18, s32[1,128]{1,0:T(1,128)} %bitcast.21, bf16[3,3,64]{2,1,0:T(4,128)(2,1)} %bitcast.17, bf16[3,3,64,64]{3,2,1,0:T(8,128)(2,1)} %bitcast.16, ...), custom_call_target="tpu_custom_call" | custom-call | tf_op jit(solution)/shard_map/encode/pallas_call | solution.py:549
  49.2 1.8 %copy.15 = bf16[1,1,128,1536]{3,2,1,0:T(8,128)(2,1)} copy(bf16[1,1,128,1536]{3,2,1,0:T(8,128)(2,1)} %bitcast.14) | data formatting | bytes 786432

commit v5 on v4

--- a/solution.py
+++ b/solution.py
@@ -315,9 +315,8 @@
     def _(d):
         exchange(d).start()
 
-    for c in range(2):
-        for d in range(1, mp_count):
-            part_copy(c, d).start()
+    for d in range(1, mp_count):
+        part_copy(0, d).start()
 
     loads[5].wait()
     loads[6].wait()
@@ -350,6 +349,8 @@
         value = dot(order, raw[block * span : (block + 1) * span, :]).astype(BF16)
         for g in range(5):
             weight[256 * g + 64 * block : 256 * g + 64 * (block + 1), :] = value[64 * g : 64 * (g + 1), :]
+    for d in range(1, mp_count):
+        part_copy(1, d).start()
     shifted[:, :, 3 * N_MEL :] = jnp.zeros((3, rows, 256 - 3 * N_MEL), BF16)
     hidden[:, :384] = jnp.zeros((rows, 384), BF16)
 
@@ -382,8 +383,8 @@
         )
         for d in (1, last, 2)
     }
-    for copy in window_out.values():
-        copy.start()
+    window_out[1].start()
+    window_out[last].start()
 
     def wait_window(d):
         to_lane(windows.at[0], windows.at[d], gather_send.at[d], gather_recv.at[d], d).wait_recv()
@@ -469,12 +470,13 @@
     attend(0, contexts)
     wait_window(1)
     wait_window(last)
+    window_out[2].start()
     image = jnp.concatenate([windows[1], windows[last]], axis=0)
     convolve(per_block, 3 * per_block, image)
-    wait_window(2)
     project(per_block, 3 * per_block)
     share_contexts(1, 1)
     share_contexts(last, 2)
+    wait_window(2)
     convolve(3 * per_block, rows, windows[2])
     share_ring(0)
     project(3 * per_block, rows)

time: 51.1 us -> 50.7 us (level)
  no operation moved by 1% of the time
where the time goes in v5:
time: 50.7 us; the launch traced here: 50.6 us
  Pallas kernels  48.8 us (96%)
  local copies, waits for them, and re-layouts  1.77 us (3%)
    pallas_call x1, Pallas kernels, on_device(): pl.pallas_call(functools.partial(solution_kernel, dp_count, mp_count), ou...  48.8 us
    unnamed x1, local copies, waits for them, and re-layouts  1.77 us

profile of v5, /device:TPU:1, one launch (start us, length us, event | category | flops | bytes accessed | tf_op | source)
XLA Modules:
  0.0 50.6 jit_solution(7913907882396270363)
XLA Ops:
  0.0 48.8 %encode.1 = bf16[128,1536]{1,0:T(8,128)(2,1)} custom-call(bf16[4,41216]{1,0:T(4,128)(2,1)} %bitcast.15, s32[1,4]{1,0:T(1,128)} %bitcast.20, s32[4,64]{1,0:T(4,128)} %bitcast.18, s32[1,128]{1,0:T(1,128)} %bitcast.21, bf16[3,3,64]{2,1,0:T(4,128)(2,1)} %bitcast.17, bf16[3,3,64,64]{3,2,1,0:T(8,128)(2,1)} %bitcast.16, ...), custom_call_target="tpu_custom_call" | custom-call | tf_op jit(solution)/shard_map/encode/pallas_call | solution.py:551
  48.8 1.8 %copy.15 = bf16[1,1,128,1536]{3,2,1,0:T(8,128)(2,1)} copy(bf16[1,1,128,1536]{3,2,1,0:T(8,128)(2,1)} %bitcast.14) | data formatting | bytes 786432

commit v6 on v5

--- a/solution.py
+++ b/solution.py
@@ -230,12 +230,12 @@
 
     pl.semaphore_wait(barrier, dp_count - 1 + mp_count - 1)
 
-    def exchange(d):
+    def exchange(slab, d):
         return pltpu.make_async_remote_copy(
-            src_ref=outgoing.at[d],
-            dst_ref=incoming.at[d],
-            send_sem=exchange_send.at[d],
-            recv_sem=exchange_recv.at[d],
+            src_ref=outgoing.at[slab],
+            dst_ref=incoming.at[slab],
+            send_sem=exchange_send,
+            recv_sem=exchange_recv,
             device_id=(lax.rem(dp + d, dp_count), me),
             device_id_type=MESH,
         )
@@ -313,7 +313,7 @@
 
     @pl.loop(1, dp_count)
     def _(d):
-        exchange(d).start()
+        exchange(d, d).start()
 
     for d in range(1, mp_count):
         part_copy(0, d).start()
@@ -368,10 +368,8 @@
     to_sibling(0).start()
     pass_on(0)
 
-    @pl.loop(1, dp_count)
-    def _(d):
-        exchange(d).wait_recv()
-
+    all_slabs = exchange(pl.ds(1, dp_count - 1), 1)
+    all_slabs.wait_recv()
     for d in range(dp_count):
         slots_rows[capacity * d : capacity * (d + 1), :] = incoming[d].astype(F32)
     windows[0] = dot(take, slots_rows[...].astype(BF16)).astype(BF16)
@@ -468,6 +466,10 @@
     pass_on(1)
     project(0, per_block)
     attend(0, contexts)
+    all_slabs.wait_send()
+    for c in range(2):
+        for d in range(1, mp_count):
+            part_copy(c, d).wait_send()
     wait_window(1)
     wait_window(last)
     window_out[2].start()
@@ -482,6 +484,13 @@
     project(3 * per_block, rows)
     share_ring(1)
     share_contexts(2, 3)
+    for copy in list(window_out.values()) + [context_out[1], context_out[last]]:
+        copy.wait_send()
+    for c in range(2):
+        for step in range(2):
+            ring_copy(c, step, parity).wait_send()
+    for index in range(7):
+        to_sibling(index).wait_send()
     for index in range(7):
         to_sibling(index).wait_recv()
 
@@ -494,19 +503,7 @@
     for index, value in zip((core, 1 - core), sides):
         encoded[:, pl.ds(pl.multiple_of(index * half, 128), half)] = value.astype(BF16)
 
-    @pl.loop(1, dp_count)
-    def _(d):
-        exchange(d).wait_send()
-
-    for copy in list(window_out.values()) + list(context_out.values()):
-        copy.wait_send()
-    for c in range(2):
-        for d in range(1, mp_count):
-            part_copy(c, d).wait_send()
-        for step in range(2):
-            ring_copy(c, step, parity).wait_send()
-    for index in range(7):
-        to_sibling(index).wait_send()
+    context_out[2].wait_send()
 
 
 def on_device(
@@ -585,8 +582,8 @@
             VMEM((mp_count, per_block, local), BF16),
             VMEM((mp_count, per_block, local), BF16),
             dma((15,)),
-            dma((dp_count,)),
-            dma((dp_count,)),
+            dma,
+            dma,
             dma((mp_count,)),
             dma((mp_count,)),
             dma((2, mp_count)),

time: 50.7 us -> 49.4 us (0.974)
  Pallas kernels: 48.8 us -> 47.5 us
    pallas_call x1, Pallas kernels: 48.8 us -> 47.5 us  [on_device(): pl.pallas_call(functools.partial(solution_kernel, dp_count, mp_count), ou...]
where the time goes in v6:
time: 49.4 us; the launch traced here: 49.3 us
  Pallas kernels  47.5 us (96%)
  local copies, waits for them, and re-layouts  1.77 us (4%)
    pallas_call x1, Pallas kernels, on_device(): pl.pallas_call(functools.partial(solution_kernel, dp_count, mp_count), ou...  47.5 us
    unnamed x1, local copies, waits for them, and re-layouts  1.77 us

profile of v6, /device:TPU:1, one launch (start us, length us, event | category | flops | bytes accessed | tf_op | source)
XLA Modules:
  0.0 49.3 jit_solution(8374245392111821491)
XLA Ops:
  0.0 47.5 %encode.1 = bf16[128,1536]{1,0:T(8,128)(2,1)} custom-call(bf16[4,41216]{1,0:T(4,128)(2,1)} %bitcast.15, s32[1,4]{1,0:T(1,128)} %bitcast.20, s32[4,64]{1,0:T(4,128)} %bitcast.18, s32[1,128]{1,0:T(1,128)} %bitcast.21, bf16[3,3,64]{2,1,0:T(4,128)(2,1)} %bitcast.17, bf16[3,3,64,64]{3,2,1,0:T(8,128)(2,1)} %bitcast.16, ...), custom_call_target="tpu_custom_call" | custom-call | tf_op jit(solution)/shard_map/encode/pallas_call | solution.py:548
  47.5 1.8 %copy.15 = bf16[1,1,128,1536]{3,2,1,0:T(8,128)(2,1)} copy(bf16[1,1,128,1536]{3,2,1,0:T(8,128)(2,1)} %bitcast.14) | data formatting | bytes 786432

commit v7 on v6

--- a/solution.py
+++ b/solution.py
@@ -136,6 +136,8 @@
     far_recv,
     context_send,
     context_recv,
+    pair_send,
+    pair_recv,
 ):
     dp, me = lax.axis_index("dp"), lax.axis_index("mp")
     core = lax.rem(dp, 2)
@@ -220,9 +222,9 @@
     column = iota((slots, frames), 1)
     own = dot(one_hot(column == place), image)
     earlier = dot(one_hot(column == place - utterances), image)
-    slots_rows[...] = jnp.where(iota(own.shape, 1) < ROW, earlier, own)
+    slots_rows[...] = jnp.where(iota(own.shape, 1) < ROW, earlier, own).astype(BF16)
     for d in range(dp_count):
-        slab = slots_rows[capacity * d : capacity * (d + 1), :].astype(BF16)
+        slab = slots_rows[capacity * d : capacity * (d + 1), :]
         if d == 0:
             incoming[0] = slab
         else:
@@ -371,8 +373,8 @@
     all_slabs = exchange(pl.ds(1, dp_count - 1), 1)
     all_slabs.wait_recv()
     for d in range(dp_count):
-        slots_rows[capacity * d : capacity * (d + 1), :] = incoming[d].astype(F32)
-    windows[0] = dot(take, slots_rows[...].astype(BF16)).astype(BF16)
+        slots_rows[capacity * d : capacity * (d + 1), :] = incoming[d]
+    windows[0] = dot(take, slots_rows[...]).astype(BF16)
 
     last = mp_count - 1
     window_out = {
@@ -422,7 +424,7 @@
     lower = iota((per_block, 128), 1) < HEAD_DIM
     zero = jnp.zeros((per_block, 128), BF16)
 
-    def attend(b, target):
+    def attend(b, target, after=None):
         d = (0, 1, last, 2)[b]
         block_ids = ids[pl.ds(lax.rem(me + d, mp_count), 1), :]
         across = jnp.broadcast_to(block_ids, (per_block, per_block))
@@ -448,6 +450,8 @@
                 total = jnp.sum(exponent, axis=-1, keepdims=True)
                 weights.append((exponent / total).astype(BF16))
             target[b, :, lanes] = dot(jnp.concatenate(weights, axis=1), value_pair).astype(BF16)
+            if after is not None:
+                after(pair, lanes)
 
     context_out = {}
 
@@ -483,7 +487,18 @@
     share_ring(0)
     project(3 * per_block, rows)
     share_ring(1)
-    share_contexts(2, 3)
+
+    def pair_copy(pair, lanes):
+        return to_lane(
+            sending.at[3, :, lanes],
+            contexts.at[mp_count - 2, :, lanes],
+            pair_send.at[pair],
+            pair_recv.at[pair],
+            2,
+        )
+
+    attend(3, sending, lambda pair, lanes: pair_copy(pair, lanes).start())
+    pairs = [pair_copy(pair, slice(pair * 128, (pair + 1) * 128)) for pair in range(local // 128)]
     for copy in list(window_out.values()) + [context_out[1], context_out[last]]:
         copy.wait_send()
     for c in range(2):
@@ -496,14 +511,18 @@
 
     sides = [embedded[:per_block, pl.ds(pl.multiple_of(index * half, 128), half)].astype(F32) for index in (core, 1 - core)]
     for d in (0, 1, last, 2):
-        if d:
+        if d == 2:
+            for copy in pairs:
+                copy.wait_recv()
+        elif d:
             to_lane(sending.at[d], contexts.at[d], context_send.at[d], context_recv.at[d], d).wait_recv()
         for index, part in enumerate((near, far)):
             sides[index] += dot(contexts[d], part[d])
     for index, value in zip((core, 1 - core), sides):
         encoded[:, pl.ds(pl.multiple_of(index * half, 128), half)] = value.astype(BF16)
 
-    context_out[2].wait_send()
+    for copy in pairs:
+        copy.wait_send()
 
 
 def on_device(
@@ -569,7 +588,7 @@
             VMEM((30 * CH, 4 * CH), BF16),
             VMEM((CH * MEL_SUB, model), BF16),
             VMEM((utterances * SLOT_ROWS, 896), BF16),
-            VMEM((slots, WINDOW), F32),
+            VMEM((slots, WINDOW), BF16),
             VMEM((dp_count, capacity, WINDOW), BF16),
             VMEM((dp_count, capacity, WINDOW), BF16),
             VMEM((mp_count, per_block, WINDOW), BF16),
@@ -594,6 +613,8 @@
             dma((7,)),
             dma((mp_count,)),
             dma((mp_count,)),
+            dma((local // 128,)),
+            dma((local // 128,)),
         ],
         compiler_params=pltpu.CompilerParams(
             vmem_limit_bytes=60 * 2**20, collective_id=0, has_side_effects=True

time: 49.4 us -> 50.1 us (1.014)
  Pallas kernels: 47.5 us -> 48.2 us
    pallas_call x1, Pallas kernels: 47.5 us -> 48.2 us  [on_device(): pl.pallas_call(functools.partial(solution_kernel, dp_count, mp_count), ou...]
where the time goes in v7:
time: 50.1 us; the launch traced here: 50 us
  Pallas kernels  48.2 us (96%)
  local copies, waits for them, and re-layouts  1.77 us (4%)
    pallas_call x1, Pallas kernels, on_device(): pl.pallas_call(functools.partial(solution_kernel, dp_count, mp_count), ou...  48.2 us
    unnamed x1, local copies, waits for them, and re-layouts  1.77 us

profile of v7, /device:TPU:1, one launch (start us, length us, event | category | flops | bytes accessed | tf_op | source)
XLA Modules:
  0.0 50.0 jit_solution(4233746280629136694)
XLA Ops:
  0.0 48.2 %encode.1 = bf16[128,1536]{1,0:T(8,128)(2,1)} custom-call(bf16[4,41216]{1,0:T(4,128)(2,1)} %bitcast.15, s32[1,4]{1,0:T(1,128)} %bitcast.20, s32[4,64]{1,0:T(4,128)} %bitcast.18, s32[1,128]{1,0:T(1,128)} %bitcast.21, bf16[3,3,64]{2,1,0:T(4,128)(2,1)} %bitcast.17, bf16[3,3,64,64]{3,2,1,0:T(8,128)(2,1)} %bitcast.16, ...), custom_call_target="tpu_custom_call" | custom-call | tf_op jit(solution)/shard_map/encode/pallas_call | solution.py:567
  48.2 1.8 %copy.15 = bf16[1,1,128,1536]{3,2,1,0:T(8,128)(2,1)} copy(bf16[1,1,128,1536]{3,2,1,0:T(8,128)(2,1)} %bitcast.14) | data formatting | bytes 786432
